TPU v7x, 256 devices: a whole 4x4x8 slice. The times are simulated.
256 devices in a mesh: row: 32 (over x_lo, z, core), rep: 8 (over x_hi, y).
Axes of the slice: x: 4 (x_hi: 2, x_lo: 2; x = x_hi * 2 + x_lo), y: 4, z: 8, core: 2. Of those that a mesh axis runs over, the one named last changes fastest.
Arguments:
- node_features: bfloat16 [32768, 768], P(('row', 'rep')), may hold values from -6 to 6
- self_weight: bfloat16 [768, 256], replicated, may hold values from -0.21875 to 0.21875
- neigh_weight: bfloat16 [768, 256], replicated, may hold values from -0.21875 to 0.21875
- bias: float32 [256], replicated, may hold values from -4 to 4
- block_values: bfloat16 [32, 32, 8, 128, 128], P('row', 'rep'), as said below
- block_coords: int32 [32, 32, 8, 2], P('row', 'rep'), may hold values from 0 to 7, as said below
- block_counts: int32 [32, 32], P('row', 'rep'), may hold values from 0 to 8, as said below
- out_grad: bfloat16 [32768, 256], P(('row', 'rep')), may hold values from -6 to 6
Outputs:
- activations: bfloat16 [32768, 256], P(('row', 'rep'))
- feature_grad: bfloat16 [32768, 768], P(('row', 'rep'))
- self_grad: float32 [768, 256], replicated
- neigh_grad: float32 [768, 256], replicated
- bias_grad: float32 [256], replicated
Inputs may be any that keep to these rules, and one draw needn't show every extreme that they name: block_counts[i, j] equals block_counts[j, i]; every diagonal tile pair has all 8 slots live. `block_coords`: slot b of tile pair (j, i) has the coordinates of slot b of (i, j) swapped; for a diagonal tile pair, slot 7 - b has the coordinates of slot b swapped. `block_values`: slot b of tile pair (j, i) holds the transpose of slot b of (i, j); for a diagonal tile pair, slot 7 - b holds the transpose of slot b; so A is symmetric.
All inputs are finite; a program needn't handle non-finite values.
Results may differ from a plain program's by a relative error of at most 0.017.
Values may be sent and summed in bfloat16 or wider, within the bound.
A program may use at most 64 MiB of HBM per device.

v0:
```python
import jax
import jax.numpy as jnp
from jax import lax
from jax.sharding import PartitionSpec as P


def from_root(value, axis, source):
    kept = jnp.where(lax.axis_index(axis) == source, value, 0).astype(value.dtype)
    return lax.psum(kept, axis)


def place_blocks(product, targets, live, nblocks):
    slots = jnp.arange(nblocks, dtype=jnp.int32)
    placing = ((targets[:, None] == slots[None, :]) & live[:, None]).astype(jnp.float32)
    return jnp.einsum("bp,bkf->pkf", placing, product, precision=lax.Precision.HIGHEST)


def slot_product(values, coords, blocks):
    picked = blocks[coords[:, 1]]
    product = jnp.einsum("bkl,blf->bkf", values, picked, preferred_element_type=jnp.float32)
    return (product, coords[:, 0])


def padded_term(values, coords, count, blocks):
    product, targets = slot_product(values, coords, blocks)
    live = jnp.arange(values.shape[0], dtype=jnp.int32) < count
    return place_blocks(product, targets, live, blocks.shape[0])


def shards(
    node_features,
    self_weight,
    neigh_weight,
    bias,
    block_values,
    block_coords,
    block_counts,
    out_grad,
):
    rows = node_features.shape[0]
    sections = block_values.shape[1]
    blk_side = block_values.shape[3]
    width = self_weight.shape[1]
    replica = lax.axis_index("rep")

    def tile_term(section, incoming):
        values = block_values[0, section]
        coords = block_coords[0, section]
        count = block_counts[0, section]
        blocks = incoming.reshape(incoming.shape[0] // blk_side, blk_side, width)
        return padded_term(values, coords, count, blocks)

    transformed = jnp.dot(node_features, neigh_weight, preferred_element_type=jnp.float32).astype(
        jnp.bfloat16
    )
    trans_slab = lax.all_gather(transformed, "rep", axis=0, tiled=True)
    slab_rows = trans_slab.shape[0]
    total = jnp.zeros((slab_rows // blk_side, blk_side, width), jnp.float32)
    for number in range(sections):
        incoming = from_root(trans_slab, "row", replica * sections + number)
        total = total + tile_term(number, incoming)
    aggregate = lax.psum_scatter(
        total.reshape(slab_rows, width).astype(jnp.bfloat16), "rep", scatter_dimension=0, tiled=True
    ).astype(jnp.float32)
    pre = jnp.dot(node_features, self_weight, preferred_element_type=jnp.float32) + aggregate + bias
    sigma = jax.nn.sigmoid(pre)
    activations = (pre * sigma).astype(jnp.bfloat16)
    pre_grad = (out_grad.astype(jnp.float32) * sigma * (1.0 + pre * (1.0 - sigma))).astype(
        jnp.bfloat16
    )
    grad_slab = lax.all_gather(pre_grad, "rep", axis=0, tiled=True)
    back_total = jnp.zeros((slab_rows // blk_side, blk_side, width), jnp.float32)
    for number in range(sections):
        incoming = from_root(grad_slab, "row", replica * sections + number)
        back_total = back_total + tile_term(number, incoming)
    hidden = lax.psum_scatter(
        back_total.reshape(slab_rows, width).astype(jnp.bfloat16),
        "rep",
        scatter_dimension=0,
        tiled=True,
    )
    contract_last = (((1,), (1,)), ((), ()))
    contract_first = (((0,), (0,)), ((), ()))
    feature_grad = (
        lax.dot_general(pre_grad, self_weight, contract_last, preferred_element_type=jnp.float32)
        + lax.dot_general(hidden, neigh_weight, contract_last, preferred_element_type=jnp.float32)
    ).astype(jnp.bfloat16)
    self_part = lax.dot_general(
        node_features, pre_grad, contract_first, preferred_element_type=jnp.float32
    )
    neigh_part = lax.dot_general(
        node_features, hidden, contract_first, preferred_element_type=jnp.float32
    )
    bias_part = jnp.sum(pre_grad.astype(jnp.float32), axis=0)
    summed = lax.psum((self_part, neigh_part, bias_part), ("row", "rep"))
    scale = float(rows * lax.axis_size("row") * lax.axis_size("rep")) ** (-0.5)
    return (activations, feature_grad, summed[0] * scale, summed[1] * scale, summed[2] * scale)


def solution(mesh):
    placed = (
        P(("row", "rep"), None),
        P(),
        P(),
        P(),
        P("row", "rep", None, None, None),
        P("row", "rep", None, None),
        P("row", "rep"),
        P(("row", "rep"), None),
    )
    return jax.shard_map(
        shards,
        mesh=mesh,
        in_specs=placed,
        out_specs=(P(("row", "rep"), None), P(("row", "rep"), None), P(), P(), P()),
        check_vma=False,
    )
```

profile of v0, /device:TPU:1, one launch (start us, length us, event | category | flops | bytes accessed | tf_op | source)
XLA Modules:
  0.0 1002.9 jit_solution(4937574192602446068)
XLA Ops:
  8.6 30.4 %all_gather.6 = bf16[1024,256]{1,0:T(8,128)(2,1)S(1)} all-gather(bf16[128,256]{1,0:T(8,128)(2,1)S(1)} %convolution_convert_fusion), channel_id=1, replica_groups=mesh['row'=32,'rep'=8] {'rep'}, dimensions={0}, use_global_device_ids=true | all-gather | bytes 589824 | tf_op jit(solution)/shard_map/all_gather | solution.py:56
  47.7 229.4 %all-reduce.11.cloned.1.call-done = (bf16[8,128,256]{2,1,0:T(8,128)(2,1)}, bf16[8,128,256]{2,1,0:T(8,128)(2,1)}, bf16[8,128,256]{2,1,0:T(8,128)(2,1)}, bf16[8,128,256]{2,1,0:T(8,128)(2,1)}) async-done(((bf16[8,128,256]{2,1,0:T(8,128)(2,1)}, bf16[8,128,256]{2,1,0:T(8,128)(2,1)}, bf16[8,128,256]{2,1,0:T(8,128)(2,1)}, bf16[8,128,256]{2,1,0:T(8,128)(2,1)}), (bf16[8,128,256]{2,1,0:T(8,128)(2,1)}, ...) | async-done | bytes 2097168 | tf_op jit(solution)/shard_map/psum | solution.py:9
  277.1 1.6 gather_fusion
  279.1 1.4 copy.20
  281.4 1.4 copy.21
  283.8 1.4 copy.22
  287.3 1.9 fusion.12
  294.1 72.2 %reduce-scatter.3.cloned.1.call-done = bf16[128,256]{1,0:T(8,128)(2,1)} async-done(((bf16[1024,256]{1,0:T(8,128)(2,1)}), bf16[128,256]{1,0:T(8,128)(2,1)}) %reduce-scatter.3.cloned.1.call-update) | async-done | bytes 65552 | tf_op jit(solution)/shard_map/reduce_scatter | solution.py:62
  366.3 2.3 convert_reduce_fusion
  369.2 29.1 %all_gather.7 = bf16[1024,256]{1,0:T(8,128)(2,1)S(1)} all-gather(bf16[128,256]{1,0:T(8,128)(2,1)S(1)} %get-tuple-element.26), channel_id=1, replica_groups=mesh['row'=32,'rep'=8] {'rep'}, dimensions={0}, use_global_device_ids=true | all-gather | bytes 589824 | tf_op jit(solution)/shard_map/all_gather | solution.py:71
  398.3 1.4 broadcast_select_fusion
  399.9 235.2 %all-reduce.9.cloned.1.call-done = (bf16[8,128,256]{2,1,0:T(8,128)(2,1)}, bf16[8,128,256]{2,1,0:T(8,128)(2,1)}, bf16[8,128,256]{2,1,0:T(8,128)(2,1)}, bf16[8,128,256]{2,1,0:T(8,128)(2,1)}) async-done(((bf16[8,128,256]{2,1,0:T(8,128)(2,1)}, bf16[8,128,256]{2,1,0:T(8,128)(2,1)}, bf16[8,128,256]{2,1,0:T(8,128)(2,1)}, bf16[8,128,256]{2,1,0:T(8,128)(2,1)}), (bf16[8,128,256]{2,1,0:T(8,128)(2,1)}, ...) | async-done | bytes 2097168 | tf_op jit(solution)/shard_map/psum | solution.py:9
  635.1 1.6 gather_fusion.4
  637.7 2.3 fusion.7
  641.4 2.4 gather_fusion.6
  643.9 1.4 fusion.18
  645.2 1.4 copy.26
  646.6 2.4 gather_fusion.7
  649.0 1.4 fusion.14
  651.1 1.9 convolution_add_fusion.2
  657.4 70.2 %reduce-scatter.5.cloned.1.call-done = bf16[128,256]{1,0:T(8,128)(2,1)} async-done(((bf16[1024,256]{1,0:T(8,128)(2,1)}), bf16[128,256]{1,0:T(8,128)(2,1)}) %reduce-scatter.5.cloned.1.call-update) | async-done | bytes 65552 | tf_op jit(solution)/shard_map/reduce_scatter | solution.py:76
  727.5 2.0 convolution_bitcast_fusion
  730.2 77.4 %psum.87 = f32[256]{0:T(256)S(1)} all-reduce(f32[256]{0:T(256)S(1)} %copy-done.33), channel_id=1, replica_groups=mesh['row'=32,'rep'=8] {'row','rep'}, use_global_device_ids=true, to_apply=%region_13.14 | all-reduce | flops 256 | bytes 2048 | tf_op jit(solution)/shard_map/psum | solution.py:95
  810.1 182.7 %all-reduce.7.cloned.1.call-done = (f32[768,256]{0,1:T(8,128)}, f32[768,256]{0,1:T(8,128)}) async-done(((f32[768,256]{0,1:T(8,128)}, f32[768,256]{0,1:T(8,128)}), (f32[768,256]{0,1:T(8,128)}, f32[768,256]{0,1:T(8,128)})) %all-reduce.7.cloned.1.call-update) | async-done | bytes 1572880 | tf_op jit(solution)/shard_map/psum | solution.py:95
  (125 shorter events, 34.1 us)
Async XLA Ops:
  7.2 359.1 %copy-start = (bf16[768,256]{1,0:T(8,128)(2,1)S(1)}, bf16[768,256]{1,0:T(8,128)(2,1)}, u32[]{:S(2)}) copy-start(bf16[768,256]{1,0:T(8,128)(2,1)} %param.9) | copy-start | bytes 1179652
  7.2 269.9 %all-reduce.11.cloned.1.call-start = ((), (), s32[]{:S(2)}) async-start(), calls=%async_computation.6 | async-start | bytes 4194304 | tf_op jit(solution)/shard_map/psum | solution.py:9
  40.4 6.2 copy-start.25
  40.4 238.3 %copy-start.1 = (bf16[1,4,8,128,128]{4,3,2,1,0:T(8,128)(2,1)S(1)}, bf16[1,4,8,128,128]{4,3,2,1,0:T(8,128)(2,1)}, u32[]{:S(2)}) copy-start(bf16[1,4,8,128,128]{4,3,2,1,0:T(8,128)(2,1)} %param.12) | copy-start | bytes 3145732
  40.4 325.8 %reduce-scatter.3.cloned.1.call-start = ((), (), s32[]{:S(2)}) async-start(), calls=%async_computation.2 | async-start | bytes 589824 | tf_op jit(solution)/shard_map/reduce_scatter | solution.py:62
  279.1 1.4 copy-start.13
  281.4 1.4 copy-start.12
  283.8 1.4 copy-start.11
  287.3 1.9 copy-start.2
  289.9 1.2 copy-start.4
  294.0 72.3 %copy-start.5 = (bf16[128,768]{1,0:T(8,128)(2,1)S(1)}, bf16[128,768]{1,0:T(8,128)(2,1)}, u32[]{:S(2)}) copy-start(bf16[128,768]{1,0:T(8,128)(2,1)} %param.8) | copy-start | bytes 589828
  294.0 72.3 %copy-start.34 = (bf16[128,256]{1,0:T(8,128)(2,1)S(1)}, bf16[128,256]{1,0:T(8,128)(2,1)}, u32[]{:S(2)}) copy-start(bf16[128,256]{1,0:T(8,128)(2,1)} %param.15) | copy-start | bytes 196612
  294.0 72.3 %copy-start.35 = (f32[256]{0:T(256)S(1)}, f32[256]{0:T(256)}, u32[]{:S(2)}) copy-start(f32[256]{0:T(256)} %param.11) | copy-start | bytes 3076
  294.0 341.1 %all-reduce.9.cloned.1.call-start = ((), (), s32[]{:S(2)}) async-start(), calls=%async_computation.5 | async-start | bytes 4194304 | tf_op jit(solution)/shard_map/psum | solution.py:9
  399.7 327.9 %reduce-scatter.5.cloned.1.call-start = ((), (), s32[]{:S(2)}) async-start(), calls=%async_computation.3 | async-start | bytes 589824 | tf_op jit(solution)/shard_map/reduce_scatter | solution.py:76
  637.7 2.3 copy-start.14
  651.1 1.9 copy-start.3
  651.1 1.9 copy-start.22
  651.1 1.9 copy-start.29
  655.3 0.9 copy-start.10
  655.3 337.5 %all-reduce.7.cloned.1.call-start = ((), (), s32[]{:S(2)}) async-start(), calls=%async_computation.4 | async-start | bytes 3145728 | tf_op jit(solution)/shard_map/psum | solution.py:95
  808.2 1.0 copy-start.7
  808.2 1.0 copy-start.15
  994.0 1.2 copy-start.8
  (17 other events, 11.3 us)
Sparse Core Ops, SparseCore 0:
  40.5 236.5 all-reduce.10
  294.1 72.0 reduce-scatter.2
  399.8 235.2 all-reduce.8
  655.4 72.0 reduce-scatter.4
  733.5 259.2 all-reduce.6
where the time goes:
time: 1000 us
  waiting for transfers between devices  790 us (79%)
  blocking collectives  137 us (14%)
  local copies, waits for them, and re-layouts  29.2 us (3%)
  matrix products  22.1 us (2%)
  between operations  14.2 us (1%)
  other arithmetic  10.6 us (1%)
    psum x2, waiting for transfers between devices, from_root(): return lax.psum(kept, axis)  465 us
    psum x1, waiting for transfers between devices, shards(): summed = lax.psum((self_part, neigh_part, bias_part), ('row', 'rep'))  183 us
    psum x1, blocking collectives, shards(): summed = lax.psum((self_part, neigh_part, bias_part), ('row', 'rep'))  77.4 us
    reduce_scatter x1, waiting for transfers between devices, shards(): lax.psum_scatter(total.reshape(slab_rows, width).astype(jnp.bfloat16), 'r...  72.2 us
    reduce_scatter x1, waiting for transfers between devices, shards(): lax.psum_scatter(back_total.reshape(slab_rows, width).astype(jnp.bfloat16...  70.2 us
    all_gather x1, blocking collectives, shards(): trans_slab = lax.all_gather(transformed, 'rep', axis=0, tiled=True)  30.4 us
    all_gather x1, blocking collectives, shards(): grad_slab = lax.all_gather(pre_grad, 'rep', axis=0, tiled=True)  29.1 us
  transfers between devices with their start and end apart: 5, of which 5 were waited for; matrix products, arithmetic and copies ran while one was open for 1% of the time, Pallas kernels for 0%

commit v1 on v0

v1 whole, which is shorter than its diff:
```python
import jax
import jax.numpy as jnp
from jax import lax
from jax.experimental import pallas as pl
from jax.experimental.pallas import tpu as pltpu
from jax.sharding import PartitionSpec as P

MESH = pl.DeviceIdType.MESH
BF16 = jnp.bfloat16
F32 = jnp.float32
FIN, FO, BLK, SLOTS, TILES = 768, 256, 128, 8, 4
ROWS, REPS, NZ, CHIPS = 32, 8, 8, 16
PIECE = FIN // CHIPS
HALF = FO // 2
NODES = ROWS * REPS * BLK


def wait_for(ref, sem):
    pltpu.make_async_copy(ref, ref, sem).wait()


def kernel(
    x_ref, ws_ref, wn_ref, bias_ref, a_ref, coords_ref, counts_ref, og_ref,
    act_ref, fg_ref, sg_ref, ng_ref, bg_ref,
    codes, merged, dense, feats, own, acc, psend, precv, selfpre,
    halves, sibrecv, pieces, piecerecv, vown, vrecv, full, bown, brecv,
    zrecv, xrecv, crecv, asend, zsend, xsend, csend, rssend, rsrecv,
    s1send, s1recv, r1send, r1recv, p1send, p1recv, g1send, g1recv, s2send, s2recv, bsend, bread,
):
    row = lax.axis_index("row")
    rep = lax.axis_index("rep")
    core = lax.rem(row, 2)
    chip = lax.div(row, 2)
    z = lax.rem(chip, NZ)
    xlo = lax.div(chip, NZ)
    col = 2 * xlo + core

    def row_at(xl, zz, cc):
        return (xl * NZ + zz) * 2 + cc

    up = row_at(xlo, lax.rem(z + 1, NZ), core)
    down = row_at(xlo, lax.rem(z + NZ - 1, NZ), core)
    across = row_at(1 - xlo, z, core)
    sibling = row_at(xlo, z, 1 - core)
    far_row = TILES * rep + lax.rem(row, TILES)
    far_rep = lax.div(row, TILES)
    is_far = far_rep != rep

    barrier = pltpu.get_barrier_semaphore()

    def greet(to_row, to_rep):
        pl.semaphore_signal(barrier, inc=1, device_id=(to_row, to_rep), device_id_type=MESH)

    lax.fori_loop(1, REPS, lambda d, _: greet(row, lax.rem(rep + d, REPS)), None)
    lax.fori_loop(1, CHIPS, lambda d, _: greet(2 * lax.rem(chip + d, CHIPS) + core, rep), None)
    greet(sibling, rep)

    @pl.when(is_far)
    def _():
        greet(far_row, far_rep)

    own[0] = jnp.dot(x_ref[...], wn_ref[...], preferred_element_type=F32).astype(BF16)

    pl.semaphore_wait(barrier, REPS - 1 + CHIPS - 1 + 1 + jnp.where(is_far, 1, 0))

    def block_of(which, zz, cc):
        return feats.at[which, zz, pl.ds(pl.multiple_of(cc * BLK, BLK), BLK), :]

    def remote(src, dst, ssem, rsem, to_row, to_rep):
        return pltpu.make_async_remote_copy(
            src_ref=src, dst_ref=dst, send_sem=ssem, recv_sem=rsem,
            device_id=(to_row, to_rep), device_id_type=MESH,
        )

    def swap_own(which):
        far_chip = lax.div(far_row, 2)
        far_col = 2 * lax.div(far_chip, NZ) + lax.rem(far_row, 2)

        @pl.when(is_far)
        def _():
            remote(
                own.at[which], block_of(which, lax.rem(far_chip, NZ), far_col),
                asend.at[which], zrecv.at[which, 0], far_row, far_rep,
            ).start()

        @pl.when(jnp.logical_not(is_far))
        def _():
            feats[which, z, pl.ds(pl.multiple_of(col * BLK, BLK), BLK), :] = own[which]

    def group_at(event):
        hops = (event + 1) // 2
        return lax.rem(z + (NZ - hops if event % 2 else hops), NZ)

    def add_group(event, which):
        zz = group_at(event)

        def chunk(i, _):
            rows = pl.ds(pl.multiple_of(i * 256, 256), 256)
            part = jnp.dot(dense[zz, rows, :], feats[which, zz], preferred_element_type=F32)
            if event == 0:
                acc[rows, :] = part
            else:
                acc[rows, :] += part
            return None

        lax.fori_loop(0, 4, chunk, None)

    def gather(which, hooks):
        def forward(event, cc, sem_index):
            block = block_of(which, group_at(event), cc)
            remote(block, block, csend.at[which], crecv.at[which, sem_index], sibling, rep).start()

        def finish(event):
            for cc in (0, 1):
                block = block_of(which, group_at(event), 2 * cc)
                wait_for(block, crecv.at[which, 2 * event + cc])
            add_group(event, which)

        for event in range(NZ):
            block = block_of(which, group_at(event), col)
            if event == 0:
                @pl.when(is_far)
                def _():
                    wait_for(block, zrecv.at[which, 0])
            else:
                wait_for(block, zrecv.at[which, event])
            if event == 0 or (event % 2 and event < 7):
                later = 1 if event == 0 else event + 2
                remote(block, block, zsend.at[which], zrecv.at[which, later], up, rep).start()
            if event % 2 == 0 and event < 6:
                remote(block, block, zsend.at[which], zrecv.at[which, event + 2], down, rep).start()
            remote(block, block, xsend.at[which], xrecv.at[which, event], across, rep).start()
            forward(event, col, 2 * event)
            if event == 0:
                hooks.get("first", lambda: None)()
            if event >= 1:
                wait_for(block, xrecv.at[which, event - 1])
                forward(event - 1, 2 * (1 - xlo) + core, 2 * event - 1)
            if event >= 2:
                finish(event - 2)
            hooks.get(event, lambda: None)()
        wait_for(block, xrecv.at[which, NZ - 1])
        forward(NZ - 1, 2 * (1 - xlo) + core, 2 * NZ - 1)
        finish(NZ - 2)
        finish(NZ - 1)

    def scatter(which, beside):
        psend[which] = acc[...].astype(BF16).reshape(REPS, BLK, FO)

        def send(d, _):
            to = lax.rem(rep + d, REPS)
            remote(
                psend.at[which, to], precv.at[which, rep], rssend.at[which], rsrecv.at[which], row, to
            ).start()

        lax.fori_loop(1, REPS, send, None)
        beside()
        total = acc[pl.ds(pl.multiple_of(rep * BLK, BLK), BLK), :]
        wait_for(precv.at[which, pl.ds(0, REPS - 1)], rsrecv.at[which])
        for d in range(1, REPS):
            total += precv[which, lax.rem(rep + d, REPS)].astype(F32)
        return total

    def grad_start(a, left, right):
        part = lax.dot_general(left, right, (((0,), (0,)), ((), ())), preferred_element_type=F32)
        halves[a, 0] = part[:, :HALF].astype(BF16)
        halves[a, 1] = part[:, HALF:].astype(BF16)
        remote(halves.at[a, 1 - core], sibrecv.at[a], s1send.at[a], s1recv.at[a], sibling, rep).start()

    def grad_chips(a):
        wait_for(sibrecv.at[a], s1recv.at[a])
        both = halves[a, core].astype(F32) + sibrecv[a].astype(F32)
        pieces[a] = both.astype(BF16).reshape(CHIPS, PIECE, HALF)

        def send(d, _):
            to = lax.rem(chip + d, CHIPS)
            remote(
                pieces.at[a, to], piecerecv.at[a, chip], r1send.at[a], r1recv.at[a], 2 * to + core, rep
            ).start()

        lax.fori_loop(1, CHIPS, send, None)

    def grad_reps(a):
        total = pieces[a, chip].astype(F32)
        wait_for(piecerecv.at[a, pl.ds(0, CHIPS - 1)], r1recv.at[a])
        for d in range(1, CHIPS):
            total += piecerecv[a, lax.rem(chip + d, CHIPS)].astype(F32)
        vown[a] = total

        def send(d, _):
            remote(
                vown.at[a], vrecv.at[a, rep], p1send.at[a], p1recv.at[a], row, lax.rem(rep + d, REPS)
            ).start()

        lax.fori_loop(1, REPS, send, None)

    def grad_hand_out(a):
        wait_for(vrecv.at[a, pl.ds(0, REPS - 1)], p1recv.at[a])
        vrecv[a, rep] = vown[a]
        total = vrecv[a, 0]
        for q in range(1, REPS):
            total += vrecv[a, q]
        full[a, core, chip] = total.astype(BF16)

        def send(d, _):
            piece = full.at[a, core, chip]
            to = lax.rem(chip + d, CHIPS)
            remote(piece, piece, g1send.at[a], g1recv.at[a], 2 * to + core, rep).start()

        lax.fori_loop(1, CHIPS, send, None)

    def grad_share(a):
        wait_for(full.at[a, core, pl.ds(0, CHIPS - 1)], g1recv.at[a])
        half = full.at[a, core]
        remote(half, half, s2send.at[a], s2recv.at[a], sibling, rep).start()

    def grad_end(a, out_ref):
        wait_for(full.at[a, 1 - core], s2recv.at[a])
        for h in (0, 1):
            out_ref[:, h * HALF:(h + 1) * HALF] = full[a, h].reshape(FIN, HALF).astype(F32) * (NODES ** -0.5)

    def grad_drain(a):
        wait_for(sibrecv.at[a], s1send.at[a])
        wait_for(piecerecv.at[a, pl.ds(0, CHIPS - 1)], r1send.at[a])
        wait_for(vrecv.at[a, pl.ds(0, REPS - 1)], p1send.at[a])
        wait_for(full.at[a, core, pl.ds(0, CHIPS - 1)], g1send.at[a])
        wait_for(full.at[a, core], s2send.at[a])

    def lay_out_strip():
        def merge(k, _):
            for b in range(SLOTS):
                where = coords_ref[0, k, b, 0] * SLOTS + coords_ref[0, k, b, 1]
                codes[k * SLOTS + b] = jnp.where(b < counts_ref[0, k], where, 255)
            for b in range(SLOTS):
                total = a_ref[0, k, b].astype(F32)
                for other in range(b):
                    same = codes[k * SLOTS + other] == codes[k * SLOTS + b]
                    total += a_ref[0, k, other].astype(F32) * jnp.where(same, 1.0, 0.0)
                merged[k, b] = total.astype(BF16)
            merged[k, SLOTS] = jnp.zeros((BLK, BLK), BF16)
            return None

        lax.fori_loop(0, TILES, merge, None)

        def place(zz, _):
            for cc in range(4):
                k = 2 * lax.rem(zz, 2) + cc % 2
                q = 4 * (cc // 2) + lax.div(zz, 2)
                for i in range(SLOTS):
                    slot = SLOTS
                    for b in range(SLOTS):
                        slot = jnp.where(codes[k * SLOTS + b] == i * SLOTS + q, b, slot)
                    dense[zz, i * BLK:(i + 1) * BLK, cc * BLK:(cc + 1) * BLK] = merged[k, slot]
            return None

        lax.fori_loop(0, NZ, place, None)

    def while_swapping():
        lay_out_strip()
        selfpre[...] = jnp.dot(x_ref[...], ws_ref[...], preferred_element_type=F32) + bias_ref[...]

    swap_own(0)
    gather(0, {"first": while_swapping})
    pre = selfpre[...] + scatter(0, lambda: None)
    sigma = jax.nn.sigmoid(pre)
    act_ref[...] = (pre * sigma).astype(BF16)
    own[1] = (og_ref[...].astype(F32) * sigma * (1.0 + pre * (1.0 - sigma))).astype(BF16)
    swap_own(1)
    grad_start(0, x_ref[...], own[1])

    gather(1, {
        "first": lambda: grad_chips(0),
        4: lambda: grad_reps(0),
        7: lambda: grad_hand_out(0),
    })

    def bias_part():
        total = jnp.zeros((8, FO), F32)
        ones = jnp.ones((8, 4 * BLK), BF16)
        for zz in range(NZ):
            total += jnp.dot(ones, feats[1, zz], preferred_element_type=F32)
        bown[...] = total

        def send(d, _):
            remote(bown, brecv.at[rep], bsend, bread, row, lax.rem(rep + d, REPS)).start()

        lax.fori_loop(1, REPS, send, None)
        grad_share(0)

    hidden = scatter(1, bias_part).astype(BF16)
    grad_start(1, x_ref[...], hidden)
    last = (((1,), (1,)), ((), ()))
    fg_ref[...] = (
        lax.dot_general(own[1], ws_ref[...], last, preferred_element_type=F32)
        + lax.dot_general(hidden, wn_ref[...], last, preferred_element_type=F32)
    ).astype(BF16)
    grad_chips(1)
    wait_for(brecv.at[pl.ds(0, REPS - 1)], bread)
    brecv[rep] = bown[...]
    total = brecv[0, 0:1, :]
    for q in range(1, REPS):
        total += brecv[q, 0:1, :]
    bg_ref[...] = total * (NODES ** -0.5)
    grad_end(0, sg_ref)
    grad_reps(1)
    grad_hand_out(1)
    for which in (0, 1):
        @pl.when(is_far)
        def _():
            wait_for(own.at[which], asend.at[which])

        wait_for(feats.at[which, pl.ds(0, 7), pl.ds(0, BLK), :], zsend.at[which])
        wait_for(feats.at[which, :, pl.ds(0, BLK), :], xsend.at[which])
        wait_for(feats.at[which, :, pl.ds(0, 2 * BLK), :], csend.at[which])
        wait_for(psend.at[which, pl.ds(0, REPS - 1)], rssend.at[which])
    wait_for(brecv.at[pl.ds(0, REPS - 1)], bsend)
    grad_drain(0)
    grad_share(1)
    grad_end(1, ng_ref)
    grad_drain(1)


def shards(node_features, self_weight, neigh_weight, bias, block_values, block_coords, block_counts, out_grad):
    vmem = pl.BlockSpec(memory_space=pltpu.VMEM)
    smem = pl.BlockSpec(memory_space=pltpu.SMEM)
    dma = pltpu.SemaphoreType.DMA
    outs = pl.pallas_call(
        kernel,
        out_shape=(
            jax.ShapeDtypeStruct((BLK, FO), BF16),
            jax.ShapeDtypeStruct((BLK, FIN), BF16),
            jax.ShapeDtypeStruct((FIN, FO), F32),
            jax.ShapeDtypeStruct((FIN, FO), F32),
            jax.ShapeDtypeStruct((1, FO), F32),
        ),
        in_specs=[vmem, vmem, vmem, vmem, vmem, smem, smem, vmem],
        out_specs=(vmem,) * 5,
        scratch_shapes=[
            pltpu.SMEM((TILES * SLOTS,), jnp.int32),
            pltpu.VMEM((TILES, SLOTS + 1, BLK, BLK), BF16),
            pltpu.VMEM((NZ, SLOTS * BLK, 4 * BLK), BF16),
            pltpu.VMEM((2, NZ, 4 * BLK, FO), BF16),
            pltpu.VMEM((2, BLK, FO), BF16),
            pltpu.VMEM((SLOTS * BLK, FO), F32),
            pltpu.VMEM((2, REPS, BLK, FO), BF16),
            pltpu.VMEM((2, REPS, BLK, FO), BF16),
            pltpu.VMEM((BLK, FO), F32),
            pltpu.VMEM((2, 2, FIN, HALF), BF16),
            pltpu.VMEM((2, FIN, HALF), BF16),
            pltpu.VMEM((2, CHIPS, PIECE, HALF), BF16),
            pltpu.VMEM((2, CHIPS, PIECE, HALF), BF16),
            pltpu.VMEM((2, PIECE, HALF), F32),
            pltpu.VMEM((2, REPS, PIECE, HALF), F32),
            pltpu.VMEM((2, 2, CHIPS, PIECE, HALF), BF16),
            pltpu.VMEM((8, FO), F32),
            pltpu.VMEM((REPS, 8, FO), F32),
            dma((2, NZ)), dma((2, NZ)), dma((2, 2 * NZ)),
            dma((2,)), dma((2,)), dma((2,)), dma((2,)), dma((2,)), dma((2,)),
            dma((2,)), dma((2,)), dma((2,)), dma((2,)), dma((2,)),
            dma((2,)), dma((2,)), dma((2,)), dma((2,)), dma((2,)),
            dma, dma,
        ],
        compiler_params=pltpu.CompilerParams(
            collective_id=0, has_side_effects=True, vmem_limit_bytes=48 * 1024 * 1024
        ),
        cost_estimate=pl.CostEstimate(flops=5 * 10 ** 9, bytes_accessed=6 * 10 ** 6, transcendentals=BLK * FO),
        name="sage_layer",
    )(
        node_features, self_weight, neigh_weight, bias.reshape(1, FO), block_values, block_coords, block_counts,
        out_grad,
    )
    return outs[:4] + (outs[4].reshape(FO),)


def solution(mesh):
    nodes = P(("row", "rep"), None)
    placed = (
        nodes, P(), P(), P(), P("row", "rep", None, None, None), P("row", "rep", None, None), P("row", "rep"), nodes,
    )
    return jax.shard_map(
        shards, mesh=mesh, in_specs=placed, out_specs=(nodes, nodes, P(), P(), P()), check_vma=False
    )
```

time: 1000 us -> 132 us (0.13)
  waiting for transfers between devices: 790 us -> 0 us
  blocking collectives: 137 us -> 0 us
  Pallas kernels: 0 us -> 121 us
  matrix products: 22.1 us -> 0 us
  local copies, waits for them, and re-layouts: 29.2 us -> 9.41 us
  between operations: 14.2 us -> 0.66 us
  other arithmetic: 10.6 us -> 0 us
    psum x3 -> x0, waiting for transfers between devices: 647 us -> none  [the longest x2 465 us: from_root(): return lax.psum(kept, axis)]
    reduce_scatter x2 -> x0, waiting for transfers between devices: 142 us -> none  [the longest x1 72.2 us: shards(): lax.psum_scatter(total.reshape(slab_rows, width).astype(jnp.bfloat16), 'r...]
    pallas_call x0 -> x1, Pallas kernels: none -> 121 us  [shards(): pl.pallas_call(kernel, out_shape=(jax.ShapeDtypeStruct((BLK, FO), BF16),...]
    psum x1 -> x0, blocking collectives: 77.4 us -> none  [shards(): summed = lax.psum((self_part, neigh_part, bias_part), ('row', 'rep'))]
    all_gather x2 -> x0, blocking collectives: 59.5 us -> none  [the longest x1 30.4 us: shards(): trans_slab = lax.all_gather(transformed, 'rep', axis=0, tiled=True)]
    dot_general x22 -> x0, matrix products: 22.1 us -> none  [the longest x8 9.16 us: place_blocks(): jnp.einsum('bp,bkf->pkf', placing, product, precision=lax.Precision.HIGHEST)]
    gather x8 -> x0, local copies, waits for them, and re-layouts: 10.4 us -> none  [slot_product(): picked = blocks[coords[:, 1]]]
  transfers between devices with their start and end apart: 5 -> 0, of which waited for: 5 -> 0; matrix products, arithmetic and copies ran while one was open for 1% -> 0% of each run, Pallas kernels for 0% -> 0%
where the time goes in v1:
time: 132 us; the launch traced here: 131 us
  Pallas kernels  121 us (92%)
  local copies, waits for them, and re-layouts  9.41 us (7%)
    pallas_call x1, Pallas kernels, shards(): pl.pallas_call(kernel, out_shape=(jax.ShapeDtypeStruct((BLK, FO), BF16),...  121 us
    unnamed x20, local copies, waits for them, and re-layouts  9.41 us

profile of v1, /device:TPU:1, one launch (start us, length us, event | category | flops | bytes accessed | tf_op | source)
XLA Modules:
  0.0 131.2 jit_solution(5168898505363998500)
XLA Ops:
  0.6 0.0 copy-start.5
  0.6 0.0 copy-start.6
  0.7 0.8 copy.13.coords_ref
  1.4 0.0 copy-done.5
  1.4 0.0 copy-done.6
  1.4 0.0 copy-start
  1.4 1.2 copy-done
  2.7 0.0 copy-start.1
  2.7 1.0 copy-done.1
  3.7 0.0 copy-start.2
  3.7 1.0 copy-done.2
  4.7 0.0 copy-start.3
  4.7 0.9 copy-done.3
  5.6 0.0 copy-start.4
  5.6 0.8 copy-done.4
  6.4 121.1 %sage_layer.1 = (bf16[128,256]{1,0:T(8,128)(2,1)S(1)}, bf16[128,768]{1,0:T(8,128)(2,1)S(1)}, f32[768,256]{1,0:T(8,128)S(1)}, f32[768,256]{1,0:T(8,128)S(1)}, f32[1,256]{1,0:T(1,128)S(1)}) custom-call(bf16[128,768]{1,0:T(8,128)(2,1)S(1)} %copy-done.3, bf16[768,256]{1,0:T(8,128)(2,1)S(1)} %copy-done.1, bf16[768,256]{1,0:T(8,128)(2,1)S(1)} %copy-done.2, ...), custom_call_target="tpu_custom_call" | custom-call | flops 5000000000 | bytes 6000000 | tf_op jit(solution)/shard_map/sage_layer/pallas_call | solution.py:327
  127.6 0.6 copy.19
  128.2 0.7 copy.20
  128.9 0.9 copy.21
  129.8 0.9 copy.22
  130.6 0.6 copy.23
Async XLA Ops:
  0.6 0.8 copy-start.5
  0.6 0.8 copy-start.6
  1.4 1.2 copy-start
  2.7 1.0 copy-start.1
  3.7 1.0 copy-start.2
  4.7 0.9 copy-start.3
  5.6 0.8 copy-start.4

commit v2 on v1

v2 whole, which is shorter than its diff:
```python
import jax
import jax.numpy as jnp
from jax import lax
from jax.experimental import pallas as pl
from jax.experimental.pallas import tpu as pltpu
from jax.sharding import PartitionSpec as P

MESH = pl.DeviceIdType.MESH
BF16 = jnp.bfloat16
F32 = jnp.float32
FIN, FO, BLK, SLOTS, TILES = 768, 256, 128, 8, 4
ROWS, REPS, NY, NZ, CHIPS = 32, 8, 4, 8, 16
HALF = FO // 2
CHUNK = FIN // REPS
PIECE = 16
OWNERS = CHUNK // PIECE
NODES = ROWS * REPS * BLK
Z_STEP = ((0, 1), (0, -1), (1, 1), (1, -1), (0, 2), (0, -2))


def wait_for(ref, sem):
    pltpu.make_async_copy(ref, ref, sem).wait()


def kernel(
    x_hbm, ws_hbm, wn_hbm, bias_hbm, a_hbm, coords_ref, counts_ref, og_hbm,
    act_ref, fg_ref, sg_ref, ng_ref, bg_ref,
    x_ref, ws_ref, wn_ref, bias_ref, a_ref, og_ref, insem,
    codes, merged, dense, units, own, acc, psend, precv, selfpre,
    halves, sibrecv, chunks, chunkrecv, pieces, piecerecv, full, bown, brecv,
    arecv, urecv, crecv, asend, xsend, zsend, dsend, csend, rssend, rsrecv,
    s1send, s1recv, p1send, p1recv, r1send, r1recv, g1send, g1recv, q1send, q1recv, s2send, s2recv, bsend, bread,
):
    row = lax.axis_index("row")
    rep = lax.axis_index("rep")
    core = lax.rem(row, 2)
    chip = lax.div(row, 2)
    z = lax.rem(chip, NZ)
    xlo = lax.div(chip, NZ)
    xhi = lax.div(rep, NY)
    y = lax.rem(rep, NY)

    def row_at(xl, zz, cc):
        return (xl * NZ + zz) * 2 + cc

    def around(zz):
        return lax.rem(zz + 2 * NZ, NZ)

    across = row_at(1 - xlo, z, core)
    sibling = row_at(xlo, z, 1 - core)

    home = around(z + 2 * y)
    goal_rep = xlo * NY + lax.div(z, 2)
    origin_z = 2 * y + lax.rem(z, 2)

    def goal(k, h):
        return row_at(xhi, around(home + 4 * k), h)

    def origin(k, cc):
        return row_at(xhi, origin_z, cc), xlo * NY + lax.rem(lax.div(around(z - 4 * k - origin_z), 2), NY)

    def elsewhere(to_row, to_rep):
        return jnp.logical_or(to_row != row, to_rep != rep)

    barrier = pltpu.get_barrier_semaphore()

    def greet(to_row, to_rep):
        pl.semaphore_signal(barrier, inc=1, device_id=(to_row, to_rep), device_id_type=MESH)

    lax.fori_loop(1, REPS, lambda d, _: greet(row, lax.rem(rep + d, REPS)), None)
    lax.fori_loop(1, CHIPS, lambda d, _: greet(2 * lax.rem(chip + d, CHIPS) + core, rep), None)
    greet(sibling, rep)
    goals = 0
    for k in (0, 1):
        for h in (0, 1):
            from_row, from_rep = origin(k, h)

            @pl.when(elsewhere(from_row, from_rep))
            def _():
                greet(from_row, from_rep)

            goals += jnp.where(elsewhere(goal(k, h), goal_rep), 1, 0)

    inputs = [
        pltpu.make_async_copy(src, dst, insem.at[i])
        for i, (src, dst) in enumerate((
            (x_hbm, x_ref), (wn_hbm, wn_ref), (a_hbm, a_ref), (ws_hbm, ws_ref), (og_hbm, og_ref), (bias_hbm, bias_ref),
        ))
    ]
    for copy in inputs:
        copy.start()
    for copy in inputs[:2]:
        copy.wait()

    def keep(which, value):
        own[which, 0] = value[:, :HALF]
        own[which, 1] = value[:, HALF:]

    keep(0, jnp.dot(x_ref[...], wn_ref[...], preferred_element_type=F32).astype(BF16))

    pl.semaphore_wait(barrier, REPS - 1 + CHIPS - 1 + 1 + goals)

    def remote(src, dst, ssem, rsem, to_row, to_rep):
        return pltpu.make_async_remote_copy(
            src_ref=src, dst_ref=dst, send_sem=ssem, recv_sem=rsem,
            device_id=(to_row, to_rep), device_id_type=MESH,
        )

    def swap_own(which):
        place = pl.ds(pl.multiple_of(core * BLK, BLK), BLK)
        for k in (0, 1):
            for h in (0, 1):
                far = elsewhere(goal(k, h), goal_rep)

                @pl.when(far)
                def _():
                    remote(
                        own.at[which, h], units.at[which, h, xhi, home, place, :],
                        asend.at[which, 2 * k + h], arecv.at[which, 2 * k + core], goal(k, h), goal_rep,
                    ).start()

                @pl.when(jnp.logical_not(far))
                def _():
                    units[which, h, xhi, home, place, :] = own[which, h]

    def column(peer):
        return 1 - xlo if peer else xlo

    def gather(which, hooks):
        def unit(peer, offset, h):
            return units.at[which, h, column(peer), around(z + offset)]

        def arrival(peer, offset):
            return urecv.at[which, 8 * peer + offset % NZ]

        def share(peer, offset):
            piece = unit(peer, offset, core)
            remote(piece, piece, csend.at[which], crecv.at[which, 8 * peer + offset % NZ], sibling, rep).start()

        def step_z(peer, sem):
            for held, distance in Z_STEP:
                piece = unit(peer, 4 * held, core)
                to = row_at(xlo, around(z + distance), core)
                remote(piece, piece, sem, arrival(peer, 4 * held - distance), to, rep).start()

        def step_x(offset, sem):
            piece = unit(0, offset, core)
            remote(piece, piece, sem, arrival(1, offset), across, rep).start()

        first = [True]

        def add_unit(peer, offset):
            wait_for(unit(peer, offset, core), crecv.at[which, 8 * peer + offset % NZ])
            both = jnp.concatenate([unit(peer, offset, 0)[...], unit(peer, offset, 1)[...]], axis=1)
            part = jnp.dot(dense[column(peer), around(z + offset)], both, preferred_element_type=F32)
            if first[0]:
                acc[...] = part
            else:
                acc[...] += part
            first[0] = False

        def hook(name):
            hooks.get(name, lambda: None)()

        for k in (0, 1):
            for cc in (0, 1):
                @pl.when(elsewhere(*origin(k, cc)))
                def _():
                    wait_for(own.at[which, 0], arecv.at[which, 2 * k + cc])
        step_x(0, xsend.at[which])
        step_x(4, xsend.at[which])
        step_z(0, zsend.at[which])
        share(0, 0)
        share(0, 4)
        hook("swapped")
        for offset in (0, 4):
            wait_for(unit(1, offset, core), arrival(1, offset))

        @pl.when(core == 0)
        def _():
            step_z(1, dsend.at[which])

        share(1, 0)
        share(1, 4)
        offsets = [4 * held - distance for held, distance in Z_STEP]
        for offset in offsets:
            wait_for(unit(0, offset, core), arrival(0, offset))

            @pl.when(core == 1)
            def _():
                step_x(offset, dsend.at[which])

            share(0, offset)
        hook("stepped")
        rest = [(0, 0), (0, 4), (1, 0), (1, 4)] + [(0, offset) for offset in offsets]
        for i, offset in enumerate(offsets):
            for peer, earlier in rest[2 * i:2 * i + 2]:
                add_unit(peer, earlier)
            wait_for(unit(1, offset, core), arrival(1, offset))
            share(1, offset)
        hook("gathered")
        for offset in offsets:
            add_unit(1, offset)

    def scatter(which, beside):
        psend[which] = acc[...].astype(BF16).reshape(REPS, BLK, FO)

        def send(d, _):
            to = lax.rem(rep + d, REPS)
            remote(
                psend.at[which, to], precv.at[which, rep], rssend.at[which], rsrecv.at[which], row, to
            ).start()

        lax.fori_loop(1, REPS, send, None)
        beside()
        total = acc[pl.ds(pl.multiple_of(rep * BLK, BLK), BLK), :]
        wait_for(precv.at[which, pl.ds(0, REPS - 1)], rsrecv.at[which])
        for d in range(1, REPS):
            total += precv[which, lax.rem(rep + d, REPS)].astype(F32)
        return total

    def grad_start(a, left, right):
        part = lax.dot_general(left, right, (((0,), (0,)), ((), ())), preferred_element_type=F32)
        halves[a, 0] = part[:, :HALF].astype(BF16)
        halves[a, 1] = part[:, HALF:].astype(BF16)
        remote(halves.at[a, 1 - core], sibrecv.at[a], s1send.at[a], s1recv.at[a], sibling, rep).start()

    def grad_to_reps(a):
        wait_for(sibrecv.at[a], s1recv.at[a])
        both = halves[a, core].astype(F32) + sibrecv[a].astype(F32)
        chunks[a] = both.astype(BF16).reshape(REPS, CHUNK, HALF)

        def send(d, _):
            to = lax.rem(rep + d, REPS)
            remote(chunks.at[a, to], chunkrecv.at[a, rep], p1send.at[a], p1recv.at[a], row, to).start()

        lax.fori_loop(1, REPS, send, None)

    def grad_to_plane(a):
        total = chunks[a, rep].astype(F32)
        wait_for(chunkrecv.at[a, pl.ds(0, REPS - 1)], p1recv.at[a])
        for d in range(1, REPS):
            total += chunkrecv[a, lax.rem(rep + d, REPS)].astype(F32)
        pieces[a] = total.astype(BF16).reshape(OWNERS, PIECE, HALF)

        def send(d, _):
            to = lax.rem(chip + d, CHIPS)
            owner = lax.rem(to, NZ)

            @pl.when(owner < OWNERS)
            def _():
                remote(
                    pieces.at[a, owner], piecerecv.at[a, chip], r1send.at[a], r1recv.at[a], 2 * to + core, rep
                ).start()

        lax.fori_loop(1, CHIPS, send, None)

    def grad_from_plane(a):
        @pl.when(z < OWNERS)
        def _():
            wait_for(piecerecv.at[a, pl.ds(0, CHIPS - 1)], r1recv.at[a])
            piecerecv[a, chip] = pieces[a, z]
            total = piecerecv[a, 0].astype(F32)
            for m in range(1, CHIPS):
                total += piecerecv[a, m].astype(F32)
            full[a, core, rep, z] = total.astype(BF16)

            def send(d, _):
                piece = full.at[a, core, rep, z]
                to = row_at(xlo, lax.rem(z + d, NZ), core)
                remote(piece, piece, g1send.at[a], g1recv.at[a], to, rep).start()

            lax.fori_loop(1, NZ, send, None)

    def grad_from_reps(a):
        @pl.when(z < OWNERS)
        def _():
            wait_for(full.at[a, core, rep, pl.ds(0, OWNERS - 1)], g1recv.at[a])

        @pl.when(z >= OWNERS)
        def _():
            wait_for(full.at[a, core, rep], g1recv.at[a])

        def send(d, _):
            chunk = full.at[a, core, rep]
            remote(chunk, chunk, q1send.at[a], q1recv.at[a], row, lax.rem(rep + d, REPS)).start()

        lax.fori_loop(1, REPS, send, None)

    def grad_share(a):
        wait_for(full.at[a, core, pl.ds(0, REPS - 1)], q1recv.at[a])
        half = full.at[a, core]
        remote(half, half, s2send.at[a], s2recv.at[a], sibling, rep).start()

    def grad_end(a, out_ref):
        wait_for(full.at[a, 1 - core], s2recv.at[a])
        for h in (0, 1):
            out_ref[:, h * HALF:(h + 1) * HALF] = full[a, h].reshape(FIN, HALF).astype(F32) * (NODES ** -0.5)

    def grad_drain(a):
        wait_for(sibrecv.at[a], s1send.at[a])
        wait_for(chunkrecv.at[a, pl.ds(0, REPS - 1)], p1send.at[a])

        @pl.when(z < OWNERS)
        def _():
            wait_for(piecerecv.at[a, pl.ds(0, 2 * OWNERS - 1)], r1send.at[a])
            wait_for(piecerecv.at[a, pl.ds(0, NZ - 1)], g1send.at[a])

        @pl.when(z >= OWNERS)
        def _():
            wait_for(piecerecv.at[a, pl.ds(0, 2 * OWNERS)], r1send.at[a])

        wait_for(full.at[a, core, pl.ds(0, REPS - 1)], q1send.at[a])
        wait_for(full.at[a, core], s2send.at[a])

    def lay_out_strip():
        inputs[2].wait()

        def merge(k, _):
            for b in range(SLOTS):
                where = coords_ref[0, k, b, 0] * SLOTS + coords_ref[0, k, b, 1]
                codes[k * SLOTS + b] = jnp.where(b < counts_ref[0, k], where, 255)
            for b in range(SLOTS):
                total = a_ref[0, k, b].astype(F32)
                for other in range(b):
                    same = codes[k * SLOTS + other] == codes[k * SLOTS + b]
                    total += a_ref[0, k, other].astype(F32) * jnp.where(same, 1.0, 0.0)
                merged[k, b] = total.astype(BF16)
            merged[k, SLOTS] = jnp.zeros((BLK, BLK), BF16)
            return None

        lax.fori_loop(0, TILES, merge, None)

        def place(zz, _):
            parity = lax.rem(zz, 2)
            from_y = lax.rem(lax.div(around(zz - 2 * y - parity), 2), NY)
            for xl in (0, 1):
                q = NY * xl + from_y
                for cc in (0, 1):
                    k = 2 * parity + cc
                    for i in range(SLOTS):
                        slot = SLOTS
                        for b in range(SLOTS):
                            slot = jnp.where(codes[k * SLOTS + b] == i * SLOTS + q, b, slot)
                        dense[xl, zz, i * BLK:(i + 1) * BLK, cc * BLK:(cc + 1) * BLK] = merged[k, slot]
            return None

        lax.fori_loop(0, NZ, place, None)

    swap_own(0)
    lay_out_strip()
    for copy in inputs[3:]:
        copy.wait()
    selfpre[...] = jnp.dot(x_ref[...], ws_ref[...], preferred_element_type=F32) + bias_ref[...]
    gather(0, {})
    pre = selfpre[...] + scatter(0, lambda: None)
    sigma = jax.nn.sigmoid(pre)
    pre_grad = (og_ref[...].astype(F32) * sigma * (1.0 + pre * (1.0 - sigma))).astype(BF16)
    keep(1, pre_grad)
    swap_own(1)
    act_ref[...] = (pre * sigma).astype(BF16)
    grad_start(0, x_ref[...], pre_grad)
    fg_self = lax.dot_general(pre_grad, ws_ref[...], (((1,), (1,)), ((), ())), preferred_element_type=F32)
    grad_to_reps(0)

    gather(1, {
        "swapped": lambda: grad_to_plane(0),
        "stepped": lambda: grad_from_plane(0),
        "gathered": lambda: grad_from_reps(0),
    })

    def beside_scatter():
        total = jnp.zeros((8, FO), F32)
        ones = jnp.ones((8, 2 * BLK), BF16)
        for xl in (0, 1):
            for zz in range(NZ):
                both = jnp.concatenate([units[1, 0, xl, zz], units[1, 1, xl, zz]], axis=1)
                total += jnp.dot(ones, both, preferred_element_type=F32)
        bown[...] = total

        def send(d, _):
            remote(bown, brecv.at[rep], bsend, bread, row, lax.rem(rep + d, REPS)).start()

        lax.fori_loop(1, REPS, send, None)
        grad_share(0)
        grad_end(0, sg_ref)

    hidden = scatter(1, beside_scatter).astype(BF16)
    grad_start(1, x_ref[...], hidden)
    fg_ref[...] = (
        fg_self + lax.dot_general(hidden, wn_ref[...], (((1,), (1,)), ((), ())), preferred_element_type=F32)
    ).astype(BF16)
    grad_to_reps(1)
    wait_for(brecv.at[pl.ds(0, REPS - 1)], bread)
    brecv[rep] = bown[...]
    total = brecv[0, 0:1, :]
    for q in range(1, REPS):
        total += brecv[q, 0:1, :]
    bg_ref[...] = total * (NODES ** -0.5)
    grad_to_plane(1)
    grad_from_plane(1)
    for which in (0, 1):
        for k in (0, 1):
            for h in (0, 1):
                @pl.when(elsewhere(goal(k, h), goal_rep))
                def _():
                    wait_for(own.at[which, h], asend.at[which, 2 * k + h])

        wait_for(units.at[which, 0, 0, pl.ds(0, 2)], xsend.at[which])
        wait_for(units.at[which, 0, 0, pl.ds(0, 6)], zsend.at[which])
        wait_for(units.at[which, 0, 0, pl.ds(0, 6)], dsend.at[which])
        wait_for(units.at[which, 0], csend.at[which])
        wait_for(psend.at[which, pl.ds(0, REPS - 1)], rssend.at[which])
    wait_for(brecv.at[pl.ds(0, REPS - 1)], bsend)
    grad_drain(0)
    grad_from_reps(1)
    grad_share(1)
    grad_end(1, ng_ref)
    grad_drain(1)


def shards(node_features, self_weight, neigh_weight, bias, block_values, block_coords, block_counts, out_grad):
    vmem = pl.BlockSpec(memory_space=pltpu.VMEM)
    smem = pl.BlockSpec(memory_space=pltpu.SMEM)
    hbm = pl.BlockSpec(memory_space=pltpu.HBM)
    dma = pltpu.SemaphoreType.DMA
    outs = pl.pallas_call(
        kernel,
        out_shape=(
            jax.ShapeDtypeStruct((BLK, FO), BF16),
            jax.ShapeDtypeStruct((BLK, FIN), BF16),
            jax.ShapeDtypeStruct((FIN, FO), F32),
            jax.ShapeDtypeStruct((FIN, FO), F32),
            jax.ShapeDtypeStruct((1, FO), F32),
        ),
        in_specs=[hbm, hbm, hbm, hbm, hbm, smem, smem, hbm],
        out_specs=(vmem,) * 5,
        scratch_shapes=[
            pltpu.VMEM((BLK, FIN), BF16),
            pltpu.VMEM((FIN, FO), BF16),
            pltpu.VMEM((FIN, FO), BF16),
            pltpu.VMEM((1, FO), F32),
            pltpu.VMEM((1, TILES, SLOTS, BLK, BLK), BF16),
            pltpu.VMEM((BLK, FO), BF16),
            dma((6,)),
            pltpu.SMEM((TILES * SLOTS,), jnp.int32),
            pltpu.VMEM((TILES, SLOTS + 1, BLK, BLK), BF16),
            pltpu.VMEM((2, NZ, SLOTS * BLK, 2 * BLK), BF16),
            pltpu.VMEM((2, 2, 2, NZ, 2 * BLK, HALF), BF16),
            pltpu.VMEM((2, 2, BLK, HALF), BF16),
            pltpu.VMEM((SLOTS * BLK, FO), F32),
            pltpu.VMEM((2, REPS, BLK, FO), BF16),
            pltpu.VMEM((2, REPS, BLK, FO), BF16),
            pltpu.VMEM((BLK, FO), F32),
            pltpu.VMEM((2, 2, FIN, HALF), BF16),
            pltpu.VMEM((2, FIN, HALF), BF16),
            pltpu.VMEM((2, REPS, CHUNK, HALF), BF16),
            pltpu.VMEM((2, REPS, CHUNK, HALF), BF16),
            pltpu.VMEM((2, OWNERS, PIECE, HALF), BF16),
            pltpu.VMEM((2, CHIPS, PIECE, HALF), BF16),
            pltpu.VMEM((2, 2, REPS, OWNERS, PIECE, HALF), BF16),
            pltpu.VMEM((8, FO), F32),
            pltpu.VMEM((REPS, 8, FO), F32),
            dma((2, 4)), dma((2, 2 * NZ)), dma((2, 2 * NZ)), dma((2, 4)),
            dma((2,)), dma((2,)), dma((2,)), dma((2,)), dma((2,)), dma((2,)),
            dma((2,)), dma((2,)), dma((2,)), dma((2,)), dma((2,)), dma((2,)),
            dma((2,)), dma((2,)), dma((2,)), dma((2,)), dma((2,)), dma((2,)),
            dma, dma,
        ],
        compiler_params=pltpu.CompilerParams(
            collective_id=0, has_side_effects=True, vmem_limit_bytes=56 * 1024 * 1024
        ),
        cost_estimate=pl.CostEstimate(flops=5 * 10 ** 9, bytes_accessed=6 * 10 ** 6, transcendentals=BLK * FO),
        name="sage_layer",
    )(
        node_features, self_weight, neigh_weight, bias.reshape(1, FO), block_values, block_coords, block_counts,
        out_grad,
    )
    return outs[:4] + (outs[4].reshape(FO),)


def solution(mesh):
    nodes = P(("row", "rep"), None)
    placed = (
        nodes, P(), P(), P(), P("row", "rep", None, None, None), P("row", "rep", None, None), P("row", "rep"), nodes,
    )
    return jax.shard_map(
        shards, mesh=mesh, in_specs=placed, out_specs=(nodes, nodes, P(), P(), P()), check_vma=False
    )
```

time: 132 us -> 112 us (0.85)
  Pallas kernels: 121 us -> 103 us
  local copies, waits for them, and re-layouts: 9.41 us -> 8.06 us
    pallas_call x1, Pallas kernels: 121 us -> 103 us  [shards(): pl.pallas_call(kernel, out_shape=(jax.ShapeDtypeStruct((BLK, FO), BF16),...]
    unnamed x20 -> x10, local copies, waits for them, and re-layouts: 9.41 us -> 8.06 us
where the time goes in v2:
time: 112 us
  Pallas kernels  103 us (92%)
  local copies, waits for them, and re-layouts  8.06 us (7%)
    pallas_call x1, Pallas kernels, shards(): pl.pallas_call(kernel, out_shape=(jax.ShapeDtypeStruct((BLK, FO), BF16),...  103 us
    unnamed x10, local copies, waits for them, and re-layouts  8.06 us

profile of v2, /device:TPU:1, one launch (start us, length us, event | category | flops | bytes accessed | tf_op | source)
XLA Modules:
  0.0 111.5 jit_solution(13240143156472868170)
XLA Ops:
  0.6 1.4 %copy.13.coords_ref = s32[1,4,8,2]{3,2,1,0:T(8,128)} copy(s32[1,4,8,2]{2,3,1,0:T(2,128)} %param.13) | data formatting | bytes 512 | tf_op args[5]
  2.0 102.8 %sage_layer.1 = (bf16[128,256]{1,0:T(8,128)(2,1)}, bf16[128,768]{1,0:T(8,128)(2,1)}, f32[768,256]{1,0:T(8,128)}, f32[768,256]{1,0:T(8,128)}, f32[1,256]{1,0:T(1,128)}) custom-call(bf16[128,768]{1,0:T(8,128)(2,1)} %x_hbm.1, bf16[768,256]{1,0:T(8,128)(2,1)} %ws_hbm.1, bf16[768,256]{1,0:T(8,128)(2,1)} %wn_hbm.1, f32[1,256]{1,0:T(1,128)} %bitcast.3, ...), custom_call_target="tpu_custom_call" | custom-call | flops 5000000000 | bytes 6000000 | tf_op jit(solution)/shard_map/sage_layer/pallas_call | solution.py:427
  104.8 1.5 %copy.19 = bf16[128,256]{1,0:T(8,128)(2,1)} copy(bf16[128,256]{1,0:T(8,128)(2,1)} %get-tuple-element.20) | data formatting | bytes 131072
  106.3 1.6 %copy.20 = bf16[128,768]{1,0:T(8,128)(2,1)} copy(bf16[128,768]{1,0:T(8,128)(2,1)} %get-tuple-element.21) | data formatting | bytes 393216
  107.9 0.0 copy-start
  107.9 2.1 %copy.21 = f32[768,256]{1,0:T(8,128)} copy(f32[768,256]{1,0:T(8,128)} %get-tuple-element.22) | data formatting | bytes 1572864
  110.1 0.0 copy-done
  110.1 0.0 copy-start.1
  110.1 0.9 copy.22
  111.0 0.0 copy-done.1
  111.0 0.6 copy.23
Async XLA Ops:
  107.9 2.1 %copy-start = (f32[768,256]{1,0:T(8,128)S(1)}, f32[768,256]{1,0:T(8,128)}, u32[]{:S(2)}) copy-start(f32[768,256]{1,0:T(8,128)} %get-tuple-element.23) | copy-start | bytes 2359300
  110.1 0.9 copy-start.1

commit v3 on v2

--- a/solution.py
+++ b/solution.py
@@ -11,9 +11,7 @@
 FIN, FO, BLK, SLOTS, TILES = 768, 256, 128, 8, 4
 ROWS, REPS, NY, NZ, CHIPS = 32, 8, 4, 8, 16
 HALF = FO // 2
-CHUNK = FIN // REPS
-PIECE = 16
-OWNERS = CHUNK // PIECE
+PIECE = FIN // CHIPS
 NODES = ROWS * REPS * BLK
 Z_STEP = ((0, 1), (0, -1), (1, 1), (1, -1), (0, 2), (0, -2))
 
@@ -24,12 +22,12 @@
 
 def kernel(
     x_hbm, ws_hbm, wn_hbm, bias_hbm, a_hbm, coords_ref, counts_ref, og_hbm,
-    act_ref, fg_ref, sg_ref, ng_ref, bg_ref,
+    act_ref, fg_ref, full, bg_ref,
     x_ref, ws_ref, wn_ref, bias_ref, a_ref, og_ref, insem,
     codes, merged, dense, units, own, acc, psend, precv, selfpre,
-    halves, sibrecv, chunks, chunkrecv, pieces, piecerecv, full, bown, brecv,
+    halves, sibrecv, pieces, piecerecv, ringrecv, bown, brecv,
     arecv, urecv, crecv, asend, xsend, zsend, dsend, csend, rssend, rsrecv,
-    s1send, s1recv, p1send, p1recv, r1send, r1recv, g1send, g1recv, q1send, q1recv, s2send, s2recv, bsend, bread,
+    s1send, s1recv, p1send, p1recv, r1send, r1recv, q1send, q1recv, s2send, s2recv, bsend, bread,
 ):
     row = lax.axis_index("row")
     rep = lax.axis_index("rep")
@@ -49,15 +47,21 @@
     across = row_at(1 - xlo, z, core)
     sibling = row_at(xlo, z, 1 - core)
 
-    home = around(z + 2 * y)
-    goal_rep = xlo * NY + lax.div(z, 2)
-    origin_z = 2 * y + lax.rem(z, 2)
+    goal_y, odd = lax.div(z, 2), lax.rem(z, 2)
+    home = around(2 * goal_y + NY * odd + lax.rem(odd + y - goal_y + NY, NY))
+    goal_rep = xlo * NY + goal_y
 
     def goal(k, h):
         return row_at(xhi, around(home + 4 * k), h)
 
+    def maker(zz):
+        place = around(zz - 2 * y)
+        parity = lax.div(place, NY)
+        return parity, lax.rem(lax.rem(place, NY) - parity + y + NY, NY)
+
     def origin(k, cc):
-        return row_at(xhi, origin_z, cc), xlo * NY + lax.rem(lax.div(around(z - 4 * k - origin_z), 2), NY)
+        parity, from_y = maker(around(z + 4 * k))
+        return row_at(xhi, 2 * y + parity, cc), xlo * NY + from_y
 
     def elsewhere(to_row, to_rep):
         return jnp.logical_or(to_row != row, to_rep != rep)
@@ -68,7 +72,8 @@
         pl.semaphore_signal(barrier, inc=1, device_id=(to_row, to_rep), device_id_type=MESH)
 
     lax.fori_loop(1, REPS, lambda d, _: greet(row, lax.rem(rep + d, REPS)), None)
-    lax.fori_loop(1, CHIPS, lambda d, _: greet(2 * lax.rem(chip + d, CHIPS) + core, rep), None)
+    lax.fori_loop(0, REPS, lambda to, _: greet(row_at(1 - xlo, z, core), to), None)
+    lax.fori_loop(1, NZ, lambda d, _: greet(row_at(xlo, around(z + d), core), rep), None)
     greet(sibling, rep)
     goals = 0
     for k in (0, 1):
@@ -98,7 +103,7 @@
 
     keep(0, jnp.dot(x_ref[...], wn_ref[...], preferred_element_type=F32).astype(BF16))
 
-    pl.semaphore_wait(barrier, REPS - 1 + CHIPS - 1 + 1 + goals)
+    pl.semaphore_wait(barrier, REPS - 1 + REPS + NZ - 1 + 1 + goals)
 
     def remote(src, dst, ssem, rsem, to_row, to_rep):
         return pltpu.make_async_remote_copy(
@@ -122,6 +127,20 @@
                 @pl.when(jnp.logical_not(far))
                 def _():
                     units[which, h, xhi, home, place, :] = own[which, h]
+
+    others = [
+        lax.rem(xhi + dx, 2) * NY + lax.rem(y + dy, NY)
+        for dx, dy in ((1, 2), (1, 1), (1, 3), (0, 2), (1, 0), (0, 1), (0, 3))
+    ]
+
+    layer = [
+        (lax.rem(xlo + dxlo, 2), lax.rem(xhi + dxhi, 2) * NY + lax.rem(y + dy, NY))
+        for dxhi, dxlo, dy in (
+            (1, 0, 2), (1, 0, 1), (1, 0, 3), (1, 1, 2), (0, 1, 2), (1, 0, 0), (0, 0, 2), (1, 1, 1), (1, 1, 3),
+            (0, 1, 1), (0, 1, 3), (0, 0, 1), (0, 0, 3), (1, 1, 0), (0, 1, 0),
+        )
+    ]
+    mine = xlo * REPS + rep
 
     def column(peer):
         return 1 - xlo if peer else xlo
@@ -205,18 +224,15 @@
     def scatter(which, beside):
         psend[which] = acc[...].astype(BF16).reshape(REPS, BLK, FO)
 
-        def send(d, _):
-            to = lax.rem(rep + d, REPS)
+        for to in others:
             remote(
                 psend.at[which, to], precv.at[which, rep], rssend.at[which], rsrecv.at[which], row, to
             ).start()
-
-        lax.fori_loop(1, REPS, send, None)
         beside()
         total = acc[pl.ds(pl.multiple_of(rep * BLK, BLK), BLK), :]
         wait_for(precv.at[which, pl.ds(0, REPS - 1)], rsrecv.at[which])
-        for d in range(1, REPS):
-            total += precv[which, lax.rem(rep + d, REPS)].astype(F32)
+        for other in others:
+            total += precv[which, other].astype(F32)
         return total
 
     def grad_start(a, left, right):
@@ -225,92 +241,50 @@
         halves[a, 1] = part[:, HALF:].astype(BF16)
         remote(halves.at[a, 1 - core], sibrecv.at[a], s1send.at[a], s1recv.at[a], sibling, rep).start()
 
-    def grad_to_reps(a):
+    def grad_to_layer(a):
         wait_for(sibrecv.at[a], s1recv.at[a])
         both = halves[a, core].astype(F32) + sibrecv[a].astype(F32)
-        chunks[a] = both.astype(BF16).reshape(REPS, CHUNK, HALF)
-
-        def send(d, _):
-            to = lax.rem(rep + d, REPS)
-            remote(chunks.at[a, to], chunkrecv.at[a, rep], p1send.at[a], p1recv.at[a], row, to).start()
-
-        lax.fori_loop(1, REPS, send, None)
-
-    def grad_to_plane(a):
-        total = chunks[a, rep].astype(F32)
-        wait_for(chunkrecv.at[a, pl.ds(0, REPS - 1)], p1recv.at[a])
-        for d in range(1, REPS):
-            total += chunkrecv[a, lax.rem(rep + d, REPS)].astype(F32)
-        pieces[a] = total.astype(BF16).reshape(OWNERS, PIECE, HALF)
-
-        def send(d, _):
-            to = lax.rem(chip + d, CHIPS)
-            owner = lax.rem(to, NZ)
-
-            @pl.when(owner < OWNERS)
-            def _():
-                remote(
-                    pieces.at[a, owner], piecerecv.at[a, chip], r1send.at[a], r1recv.at[a], 2 * to + core, rep
-                ).start()
-
-        lax.fori_loop(1, CHIPS, send, None)
-
-    def grad_from_plane(a):
-        @pl.when(z < OWNERS)
-        def _():
-            wait_for(piecerecv.at[a, pl.ds(0, CHIPS - 1)], r1recv.at[a])
-            piecerecv[a, chip] = pieces[a, z]
-            total = piecerecv[a, 0].astype(F32)
-            for m in range(1, CHIPS):
-                total += piecerecv[a, m].astype(F32)
-            full[a, core, rep, z] = total.astype(BF16)
-
-            def send(d, _):
-                piece = full.at[a, core, rep, z]
-                to = row_at(xlo, lax.rem(z + d, NZ), core)
-                remote(piece, piece, g1send.at[a], g1recv.at[a], to, rep).start()
-
-            lax.fori_loop(1, NZ, send, None)
-
-    def grad_from_reps(a):
-        @pl.when(z < OWNERS)
-        def _():
-            wait_for(full.at[a, core, rep, pl.ds(0, OWNERS - 1)], g1recv.at[a])
-
-        @pl.when(z >= OWNERS)
-        def _():
-            wait_for(full.at[a, core, rep], g1recv.at[a])
-
-        def send(d, _):
-            chunk = full.at[a, core, rep]
-            remote(chunk, chunk, q1send.at[a], q1recv.at[a], row, lax.rem(rep + d, REPS)).start()
-
-        lax.fori_loop(1, REPS, send, None)
+        pieces[a] = both.astype(BF16).reshape(CHIPS, PIECE, HALF)
+        for xl, to in layer:
+            remote(
+                pieces.at[a, xl * REPS + to], piecerecv.at[a, mine], p1send.at[a], p1recv.at[a],
+                row_at(xl, z, core), to,
+            ).start()
+
+    def grad_to_ring(a):
+        total = pieces[a, mine].astype(F32)
+        wait_for(piecerecv.at[a, pl.ds(0, CHIPS - 1)], p1recv.at[a])
+        for xl, other in layer:
+            total += piecerecv[a, xl * REPS + other].astype(F32)
+        ringrecv[a, z] = total.astype(BF16)
+        for d in (4, 3, 5, 2, 6, 1, 7):
+            place = ringrecv.at[a, z]
+            to = row_at(xlo, around(z + d), core)
+            remote(place, place, r1send.at[a], r1recv.at[a], to, rep).start()
+
+    def grad_from_ring(a):
+        wait_for(ringrecv.at[a, pl.ds(0, NZ - 1)], r1recv.at[a])
+        total = ringrecv[a, 0].astype(F32)
+        for zz in range(1, NZ):
+            total += ringrecv[a, zz].astype(F32)
+        full[a, core, mine] = total.astype(BF16)
+        piece = full.at[a, core, mine]
+        for xl, to in layer:
+            remote(piece, piece, q1send.at[a], q1recv.at[a], row_at(xl, z, core), to).start()
 
     def grad_share(a):
-        wait_for(full.at[a, core, pl.ds(0, REPS - 1)], q1recv.at[a])
+        wait_for(full.at[a, core, pl.ds(0, CHIPS - 1)], q1recv.at[a])
         half = full.at[a, core]
         remote(half, half, s2send.at[a], s2recv.at[a], sibling, rep).start()
 
-    def grad_end(a, out_ref):
+    def grad_end(a):
         wait_for(full.at[a, 1 - core], s2recv.at[a])
-        for h in (0, 1):
-            out_ref[:, h * HALF:(h + 1) * HALF] = full[a, h].reshape(FIN, HALF).astype(F32) * (NODES ** -0.5)
 
     def grad_drain(a):
         wait_for(sibrecv.at[a], s1send.at[a])
-        wait_for(chunkrecv.at[a, pl.ds(0, REPS - 1)], p1send.at[a])
-
-        @pl.when(z < OWNERS)
-        def _():
-            wait_for(piecerecv.at[a, pl.ds(0, 2 * OWNERS - 1)], r1send.at[a])
-            wait_for(piecerecv.at[a, pl.ds(0, NZ - 1)], g1send.at[a])
-
-        @pl.when(z >= OWNERS)
-        def _():
-            wait_for(piecerecv.at[a, pl.ds(0, 2 * OWNERS)], r1send.at[a])
-
-        wait_for(full.at[a, core, pl.ds(0, REPS - 1)], q1send.at[a])
+        wait_for(piecerecv.at[a, pl.ds(0, CHIPS - 1)], p1send.at[a])
+        wait_for(ringrecv.at[a, pl.ds(0, NZ - 1)], r1send.at[a])
+        wait_for(full.at[a, core, pl.ds(0, CHIPS - 1)], q1send.at[a])
         wait_for(full.at[a, core], s2send.at[a])
 
     def lay_out_strip():
@@ -318,7 +292,7 @@
 
         def merge(k, _):
             for b in range(SLOTS):
-                where = coords_ref[0, k, b, 0] * SLOTS + coords_ref[0, k, b, 1]
+                where = coords_ref[0, k, 0, b] * SLOTS + coords_ref[0, k, 1, b]
                 codes[k * SLOTS + b] = jnp.where(b < counts_ref[0, k], where, 255)
             for b in range(SLOTS):
                 total = a_ref[0, k, b].astype(F32)
@@ -332,8 +306,7 @@
         lax.fori_loop(0, TILES, merge, None)
 
         def place(zz, _):
-            parity = lax.rem(zz, 2)
-            from_y = lax.rem(lax.div(around(zz - 2 * y - parity), 2), NY)
+            parity, from_y = maker(zz)
             for xl in (0, 1):
                 q = NY * xl + from_y
                 for cc in (0, 1):
@@ -361,12 +334,11 @@
     act_ref[...] = (pre * sigma).astype(BF16)
     grad_start(0, x_ref[...], pre_grad)
     fg_self = lax.dot_general(pre_grad, ws_ref[...], (((1,), (1,)), ((), ())), preferred_element_type=F32)
-    grad_to_reps(0)
+    grad_to_layer(0)
 
     gather(1, {
-        "swapped": lambda: grad_to_plane(0),
-        "stepped": lambda: grad_from_plane(0),
-        "gathered": lambda: grad_from_reps(0),
+        "stepped": lambda: grad_to_ring(0),
+        "gathered": lambda: grad_from_ring(0),
     })
 
     def beside_scatter():
@@ -378,27 +350,25 @@
                 total += jnp.dot(ones, both, preferred_element_type=F32)
         bown[...] = total
 
-        def send(d, _):
-            remote(bown, brecv.at[rep], bsend, bread, row, lax.rem(rep + d, REPS)).start()
-
-        lax.fori_loop(1, REPS, send, None)
-        grad_share(0)
-        grad_end(0, sg_ref)
+        for to in others:
+            remote(bown, brecv.at[rep], bsend, bread, row, to).start()
 
     hidden = scatter(1, beside_scatter).astype(BF16)
     grad_start(1, x_ref[...], hidden)
     fg_ref[...] = (
         fg_self + lax.dot_general(hidden, wn_ref[...], (((1,), (1,)), ((), ())), preferred_element_type=F32)
     ).astype(BF16)
-    grad_to_reps(1)
+    grad_to_layer(1)
+    grad_share(0)
     wait_for(brecv.at[pl.ds(0, REPS - 1)], bread)
     brecv[rep] = bown[...]
     total = brecv[0, 0:1, :]
     for q in range(1, REPS):
         total += brecv[q, 0:1, :]
-    bg_ref[...] = total * (NODES ** -0.5)
-    grad_to_plane(1)
-    grad_from_plane(1)
+    bg_ref[...] = total
+    grad_end(0)
+    grad_to_ring(1)
+    grad_from_ring(1)
     for which in (0, 1):
         for k in (0, 1):
             for h in (0, 1):
@@ -413,10 +383,19 @@
         wait_for(psend.at[which, pl.ds(0, REPS - 1)], rssend.at[which])
     wait_for(brecv.at[pl.ds(0, REPS - 1)], bsend)
     grad_drain(0)
-    grad_from_reps(1)
     grad_share(1)
-    grad_end(1, ng_ref)
+    grad_end(1)
     grad_drain(1)
+
+
+def finish(act_in, fg_in, full, bias_in, act_ref, fg_ref, sg_ref, ng_ref, bg_ref):
+    scale = NODES ** -0.5
+    for a, out_ref in enumerate((sg_ref, ng_ref)):
+        for h in (0, 1):
+            out_ref[:, h * HALF:(h + 1) * HALF] = full[a, h].reshape(FIN, HALF).astype(F32) * scale
+    act_ref[...] = act_in[...]
+    fg_ref[...] = fg_in[...]
+    bg_ref[...] = bias_in[...] * scale
 
 
 def shards(node_features, self_weight, neigh_weight, bias, block_values, block_coords, block_counts, out_grad):
@@ -429,12 +408,11 @@
         out_shape=(
             jax.ShapeDtypeStruct((BLK, FO), BF16),
             jax.ShapeDtypeStruct((BLK, FIN), BF16),
-            jax.ShapeDtypeStruct((FIN, FO), F32),
-            jax.ShapeDtypeStruct((FIN, FO), F32),
+            jax.ShapeDtypeStruct((2, 2, CHIPS, PIECE, HALF), BF16),
             jax.ShapeDtypeStruct((1, FO), F32),
         ),
         in_specs=[hbm, hbm, hbm, hbm, hbm, smem, smem, hbm],
-        out_specs=(vmem,) * 5,
+        out_specs=(vmem,) * 4,
         scratch_shapes=[
             pltpu.VMEM((BLK, FIN), BF16),
             pltpu.VMEM((FIN, FO), BF16),
@@ -454,17 +432,15 @@
             pltpu.VMEM((BLK, FO), F32),
             pltpu.VMEM((2, 2, FIN, HALF), BF16),
             pltpu.VMEM((2, FIN, HALF), BF16),
-            pltpu.VMEM((2, REPS, CHUNK, HALF), BF16),
-            pltpu.VMEM((2, REPS, CHUNK, HALF), BF16),
-            pltpu.VMEM((2, OWNERS, PIECE, HALF), BF16),
             pltpu.VMEM((2, CHIPS, PIECE, HALF), BF16),
-            pltpu.VMEM((2, 2, REPS, OWNERS, PIECE, HALF), BF16),
+            pltpu.VMEM((2, CHIPS, PIECE, HALF), BF16),
+            pltpu.VMEM((2, NZ, PIECE, HALF), BF16),
             pltpu.VMEM((8, FO), F32),
             pltpu.VMEM((REPS, 8, FO), F32),
             dma((2, 4)), dma((2, 2 * NZ)), dma((2, 2 * NZ)), dma((2, 4)),
             dma((2,)), dma((2,)), dma((2,)), dma((2,)), dma((2,)), dma((2,)),
             dma((2,)), dma((2,)), dma((2,)), dma((2,)), dma((2,)), dma((2,)),
-            dma((2,)), dma((2,)), dma((2,)), dma((2,)), dma((2,)), dma((2,)),
+            dma((2,)), dma((2,)), dma((2,)), dma((2,)),
             dma, dma,
         ],
         compiler_params=pltpu.CompilerParams(
@@ -473,10 +449,24 @@
         cost_estimate=pl.CostEstimate(flops=5 * 10 ** 9, bytes_accessed=6 * 10 ** 6, transcendentals=BLK * FO),
         name="sage_layer",
     )(
-        node_features, self_weight, neigh_weight, bias.reshape(1, FO), block_values, block_coords, block_counts,
+        node_features, self_weight, neigh_weight, bias.reshape(1, FO), block_values, block_coords.swapaxes(2, 3), block_counts,
         out_grad,
     )
-    return outs[:4] + (outs[4].reshape(FO),)
+    act, fg, sg, ng, bg = pl.pallas_call(
+        finish,
+        out_shape=(
+            jax.ShapeDtypeStruct((BLK, FO), BF16),
+            jax.ShapeDtypeStruct((BLK, FIN), BF16),
+            jax.ShapeDtypeStruct((FIN, FO), F32),
+            jax.ShapeDtypeStruct((FIN, FO), F32),
+            jax.ShapeDtypeStruct((1, FO), F32),
+        ),
+        in_specs=[vmem] * 4,
+        out_specs=(vmem,) * 5,
+        compiler_params=pltpu.CompilerParams(vmem_limit_bytes=56 * 1024 * 1024),
+        name="finish",
+    )(*outs)
+    return act, fg, sg, ng, bg.reshape(FO)
 
 
 def solution(mesh):

time: 112 us -> 97.7 us (0.87)
  local copies, waits for them, and re-layouts: 8.06 us -> 0 us
  Pallas kernels: 103 us -> 96.9 us
    pallas_call x1, Pallas kernels: 103 us -> 94.3 us  [shards(): pl.pallas_call(kernel, out_shape=(jax.ShapeDtypeStruct((BLK, FO), BF16),...]
    unnamed x10 -> x0, local copies, waits for them, and re-layouts: 8.06 us -> none
    pallas_call x0 -> x1, Pallas kernels: none -> 2.62 us  [shards(): pl.pallas_call(finish, out_shape=(jax.ShapeDtypeStruct((BLK, FO), BF16),...]
where the time goes in v3:
time: 97.7 us; the launch traced here: 97.5 us
  Pallas kernels  96.9 us (99%)
    pallas_call x1, Pallas kernels, shards(): pl.pallas_call(kernel, out_shape=(jax.ShapeDtypeStruct((BLK, FO), BF16),...  94.3 us
    pallas_call x1, Pallas kernels, shards(): pl.pallas_call(finish, out_shape=(jax.ShapeDtypeStruct((BLK, FO), BF16),...  2.62 us

profile of v3, /device:TPU:1, one launch (start us, length us, event | category | flops | bytes accessed | tf_op | source)
XLA Modules:
  0.0 97.5 jit_solution(9043026905064028960)
XLA Ops:
  0.6 94.3 %sage_layer.1 = (bf16[128,256]{1,0:T(8,128)(2,1)}, bf16[128,768]{1,0:T(8,128)(2,1)}, bf16[2,2,16,48,128]{4,3,2,1,0:T(8,128)(2,1)}, f32[1,256]{1,0:T(1,128)}) custom-call(bf16[128,768]{1,0:T(8,128)(2,1)} %x_hbm.1, bf16[768,256]{1,0:T(8,128)(2,1)} %ws_hbm.1, bf16[768,256]{1,0:T(8,128)(2,1)} %wn_hbm.1, f32[1,256]{1,0:T(1,128)} %bitcast.4, ...), custom_call_target="tpu_custom_call" | custom-call | flops 5000000000 | bytes 6000000 | tf_op jit(solution)/shard_map/sage_layer/pallas_call | solution.py:406
  94.9 2.6 %finish.1 = (bf16[128,256]{1,0:T(8,128)(2,1)}, bf16[128,768]{1,0:T(8,128)(2,1)}, f32[768,256]{1,0:T(8,128)}, f32[768,256]{1,0:T(8,128)}, f32[1,256]{1,0:T(1,128)}) custom-call(bf16[128,256]{1,0:T(8,128)(2,1)} %get-tuple-element.14.act_in, bf16[128,768]{1,0:T(8,128)(2,1)} %get-tuple-element.15.fg_in, bf16[2,2,16,48,128]{4,3,2,1,0:T(8,128)(2,1)} %get-tuple-element.16.full, ...), custom_call_target="tpu_custom_call" | custom-call | tf_op jit(solution)/shard_map/finish/pallas_call | solution.py:455

commit v4 on v3

--- a/solution.py
+++ b/solution.py
@@ -25,9 +25,10 @@
     act_ref, fg_ref, full, bg_ref,
     x_ref, ws_ref, wn_ref, bias_ref, a_ref, og_ref, insem,
     codes, merged, dense, units, own, acc, psend, precv, selfpre,
-    halves, sibrecv, pieces, piecerecv, ringrecv, bown, brecv,
+    halves, sibrecv, pieces, piecerecv, ringrecv, bown, brecv, slab,
     arecv, urecv, crecv, asend, xsend, zsend, dsend, csend, rssend, rsrecv,
     s1send, s1recv, p1send, p1recv, r1send, r1recv, q1send, q1recv, s2send, s2recv, bsend, bread,
+    slabsend, slabrecv,
 ):
     row = lax.axis_index("row")
     rep = lax.axis_index("rep")
@@ -215,28 +216,51 @@
         for i, offset in enumerate(offsets):
             for peer, earlier in rest[2 * i:2 * i + 2]:
                 add_unit(peer, earlier)
+            if i >= 2:
+                add_unit(1, offsets[i - 2])
             wait_for(unit(1, offset, core), arrival(1, offset))
             share(1, offset)
         hook("gathered")
-        for offset in offsets:
+        for offset in offsets[-2:]:
             add_unit(1, offset)
 
-    def scatter(which, beside):
+    def round_partial(which):
         psend[which] = acc[...].astype(BF16).reshape(REPS, BLK, FO)
 
+    def scatter(which):
         for to in others:
             remote(
                 psend.at[which, to], precv.at[which, rep], rssend.at[which], rsrecv.at[which], row, to
             ).start()
-        beside()
+
+    def collect(which):
         total = acc[pl.ds(pl.multiple_of(rep * BLK, BLK), BLK), :]
         wait_for(precv.at[which, pl.ds(0, REPS - 1)], rsrecv.at[which])
         for other in others:
             total += precv[which, other].astype(F32)
         return total
 
-    def grad_start(a, left, right):
-        part = lax.dot_general(left, right, (((0,), (0,)), ((), ())), preferred_element_type=F32)
+    opposite = lax.rem(xhi + 1, 2) * NY + y
+    beside = [xhi * NY + lax.rem(y + dy, NY) for dy in (2, 1, 3)]
+
+    def slab_start():
+        slab[rep] = x_ref[...].T
+        remote(slab.at[rep], slab.at[rep], slabsend, slabrecv.at[0], row, opposite).start()
+
+    def slab_own():
+        for to in beside:
+            remote(slab.at[rep], slab.at[rep], slabsend, slabrecv.at[1], row, to).start()
+
+    def slab_other():
+        wait_for(slab.at[opposite], slabrecv.at[0])
+        for to in beside:
+            remote(slab.at[opposite], slab.at[opposite], slabsend, slabrecv.at[2], row, to).start()
+
+    def slab_end():
+        wait_for(slab.at[pl.ds(0, NY - 1)], slabrecv.at[1])
+        wait_for(slab.at[pl.ds(0, NY - 1)], slabrecv.at[2])
+
+    def grad_start(a, part):
         halves[a, 0] = part[:, :HALF].astype(BF16)
         halves[a, 1] = part[:, HALF:].astype(BF16)
         remote(halves.at[a, 1 - core], sibrecv.at[a], s1send.at[a], s1recv.at[a], sibling, rep).start()
@@ -321,18 +345,23 @@
         lax.fori_loop(0, NZ, place, None)
 
     swap_own(0)
+    slab_start()
+    slab_own()
     lay_out_strip()
     for copy in inputs[3:]:
         copy.wait()
     selfpre[...] = jnp.dot(x_ref[...], ws_ref[...], preferred_element_type=F32) + bias_ref[...]
     gather(0, {})
-    pre = selfpre[...] + scatter(0, lambda: None)
+    round_partial(0)
+    scatter(0)
+    pre = selfpre[...] + collect(0)
     sigma = jax.nn.sigmoid(pre)
     pre_grad = (og_ref[...].astype(F32) * sigma * (1.0 + pre * (1.0 - sigma))).astype(BF16)
     keep(1, pre_grad)
     swap_own(1)
+    slab_other()
     act_ref[...] = (pre * sigma).astype(BF16)
-    grad_start(0, x_ref[...], pre_grad)
+    grad_start(0, jnp.dot(slab[rep], pre_grad, preferred_element_type=F32))
     fg_self = lax.dot_general(pre_grad, ws_ref[...], (((1,), (1,)), ((), ())), preferred_element_type=F32)
     grad_to_layer(0)
 
@@ -340,26 +369,36 @@
         "stepped": lambda: grad_to_ring(0),
         "gathered": lambda: grad_from_ring(0),
     })
-
-    def beside_scatter():
-        total = jnp.zeros((8, FO), F32)
-        ones = jnp.ones((8, 2 * BLK), BF16)
-        for xl in (0, 1):
-            for zz in range(NZ):
-                both = jnp.concatenate([units[1, 0, xl, zz], units[1, 1, xl, zz]], axis=1)
-                total += jnp.dot(ones, both, preferred_element_type=F32)
-        bown[...] = total
-
-        for to in others:
-            remote(bown, brecv.at[rep], bsend, bread, row, to).start()
-
-    hidden = scatter(1, beside_scatter).astype(BF16)
-    grad_start(1, x_ref[...], hidden)
+    round_partial(1)
+    slab_end()
+
+    def slab_product():
+        total = jnp.zeros((FIN, FO), F32)
+        for pair in range(REPS // 2):
+            left = jnp.concatenate([slab[2 * pair], slab[2 * pair + 1]], axis=1)
+            right = psend[1, 2 * pair:2 * pair + 2].reshape(2 * BLK, FO)
+            total += jnp.dot(left, right, preferred_element_type=F32)
+        return total
+
+    grad_start(1, slab_product())
+    grad_to_layer(1)
+    total = jnp.zeros((8, FO), F32)
+    ones = jnp.ones((8, 2 * BLK), BF16)
+    for xl in (0, 1):
+        for zz in range(NZ):
+            both = jnp.concatenate([units[1, 0, xl, zz], units[1, 1, xl, zz]], axis=1)
+            total += jnp.dot(ones, both, preferred_element_type=F32)
+    bown[...] = total
+    for to in others:
+        remote(bown, brecv.at[rep], bsend, bread, row, to).start()
+    grad_to_ring(1)
+    scatter(1)
+    grad_share(0)
+    grad_from_ring(1)
+    hidden = collect(1).astype(BF16)
     fg_ref[...] = (
         fg_self + lax.dot_general(hidden, wn_ref[...], (((1,), (1,)), ((), ())), preferred_element_type=F32)
     ).astype(BF16)
-    grad_to_layer(1)
-    grad_share(0)
     wait_for(brecv.at[pl.ds(0, REPS - 1)], bread)
     brecv[rep] = bown[...]
     total = brecv[0, 0:1, :]
@@ -367,8 +406,6 @@
         total += brecv[q, 0:1, :]
     bg_ref[...] = total
     grad_end(0)
-    grad_to_ring(1)
-    grad_from_ring(1)
     for which in (0, 1):
         for k in (0, 1):
             for h in (0, 1):
@@ -382,6 +419,7 @@
         wait_for(units.at[which, 0], csend.at[which])
         wait_for(psend.at[which, pl.ds(0, REPS - 1)], rssend.at[which])
     wait_for(brecv.at[pl.ds(0, REPS - 1)], bsend)
+    wait_for(slab.at[pl.ds(0, REPS - 1)], slabsend)
     grad_drain(0)
     grad_share(1)
     grad_end(1)
@@ -437,11 +475,12 @@
             pltpu.VMEM((2, NZ, PIECE, HALF), BF16),
             pltpu.VMEM((8, FO), F32),
             pltpu.VMEM((REPS, 8, FO), F32),
+            pltpu.VMEM((REPS, FIN, BLK), BF16),
             dma((2, 4)), dma((2, 2 * NZ)), dma((2, 2 * NZ)), dma((2, 4)),
             dma((2,)), dma((2,)), dma((2,)), dma((2,)), dma((2,)), dma((2,)),
             dma((2,)), dma((2,)), dma((2,)), dma((2,)), dma((2,)), dma((2,)),
             dma((2,)), dma((2,)), dma((2,)), dma((2,)),
-            dma, dma,
+            dma, dma, dma, dma((3,)),
         ],
         compiler_params=pltpu.CompilerParams(
             collective_id=0, has_side_effects=True, vmem_limit_bytes=56 * 1024 * 1024

time: 97.7 us -> 91.5 us (0.937)
  Pallas kernels: 96.9 us -> 90.7 us
    pallas_call x1, Pallas kernels: 94.3 us -> 88.1 us  [shards(): pl.pallas_call(kernel, out_shape=(jax.ShapeDtypeStruct((BLK, FO), BF16),...]
where the time goes in v4:
time: 91.5 us; the launch traced here: 91.4 us
  Pallas kernels  90.7 us (99%)
    pallas_call x1, Pallas kernels, shards(): pl.pallas_call(kernel, out_shape=(jax.ShapeDtypeStruct((BLK, FO), BF16),...  88.1 us
    pallas_call x1, Pallas kernels, shards(): pl.pallas_call(finish, out_shape=(jax.ShapeDtypeStruct((BLK, FO), BF16),...  2.62 us

profile of v4, /device:TPU:1, one launch (start us, length us, event | category | flops | bytes accessed | tf_op | source)
XLA Modules:
  0.0 91.4 jit_solution(9754465546791627923)
XLA Ops:
  0.6 88.1 %sage_layer.1 = (bf16[128,256]{1,0:T(8,128)(2,1)}, bf16[128,768]{1,0:T(8,128)(2,1)}, bf16[2,2,16,48,128]{4,3,2,1,0:T(8,128)(2,1)}, f32[1,256]{1,0:T(1,128)}) custom-call(bf16[128,768]{1,0:T(8,128)(2,1)} %x_hbm.1, bf16[768,256]{1,0:T(8,128)(2,1)} %ws_hbm.1, bf16[768,256]{1,0:T(8,128)(2,1)} %wn_hbm.1, f32[1,256]{1,0:T(1,128)} %bitcast.4, ...), custom_call_target="tpu_custom_call" | custom-call | flops 5000000000 | bytes 6000000 | tf_op jit(solution)/shard_map/sage_layer/pallas_call | solution.py:444
  88.8 2.6 %finish.1 = (bf16[128,256]{1,0:T(8,128)(2,1)}, bf16[128,768]{1,0:T(8,128)(2,1)}, f32[768,256]{1,0:T(8,128)}, f32[768,256]{1,0:T(8,128)}, f32[1,256]{1,0:T(1,128)}) custom-call(bf16[128,256]{1,0:T(8,128)(2,1)} %get-tuple-element.14.act_in, bf16[128,768]{1,0:T(8,128)(2,1)} %get-tuple-element.15.fg_in, bf16[2,2,16,48,128]{4,3,2,1,0:T(8,128)(2,1)} %get-tuple-element.16.full, ...), custom_call_target="tpu_custom_call" | custom-call | tf_op jit(solution)/shard_map/finish/pallas_call | solution.py:494

commit v5 on v4

--- a/solution.py
+++ b/solution.py
@@ -12,6 +12,7 @@
 ROWS, REPS, NY, NZ, CHIPS = 32, 8, 4, 8, 16
 HALF = FO // 2
 PIECE = FIN // CHIPS
+PARTS = 2
 NODES = ROWS * REPS * BLK
 Z_STEP = ((0, 1), (0, -1), (1, 1), (1, -1), (0, 2), (0, -2))
 
@@ -26,6 +27,7 @@
     x_ref, ws_ref, wn_ref, bias_ref, a_ref, og_ref, insem,
     codes, merged, dense, units, own, acc, psend, precv, selfpre,
     halves, sibrecv, pieces, piecerecv, ringrecv, bown, brecv, slab,
+    halfsend, halfrecv, halfsem,
     arecv, urecv, crecv, asend, xsend, zsend, dsend, csend, rssend, rsrecv,
     s1send, s1recv, p1send, p1recv, r1send, r1recv, q1send, q1recv, s2send, s2recv, bsend, bread,
     slabsend, slabrecv,
@@ -112,10 +114,10 @@
             device_id=(to_row, to_rep), device_id_type=MESH,
         )
 
-    def swap_own(which):
+    def swap_own(which, columns=(0, 1)):
         place = pl.ds(pl.multiple_of(core * BLK, BLK), BLK)
-        for k in (0, 1):
-            for h in (0, 1):
+        for h in columns:
+            for k in (0, 1):
                 far = elsewhere(goal(k, h), goal_rep)
 
                 @pl.when(far)
@@ -352,15 +354,24 @@
         copy.wait()
     selfpre[...] = jnp.dot(x_ref[...], ws_ref[...], preferred_element_type=F32) + bias_ref[...]
     gather(0, {})
-    round_partial(0)
-    scatter(0)
-    pre = selfpre[...] + collect(0)
-    sigma = jax.nn.sigmoid(pre)
-    pre_grad = (og_ref[...].astype(F32) * sigma * (1.0 + pre * (1.0 - sigma))).astype(BF16)
-    keep(1, pre_grad)
-    swap_own(1)
+    half_columns = [slice(h * HALF, (h + 1) * HALF) for h in (0, 1)]
+    for h, columns in enumerate(half_columns):
+        halfsend[h] = acc[:, columns].astype(BF16).reshape(REPS, BLK, HALF)
+        for to in others:
+            remote(halfsend.at[h, to], halfrecv.at[h, rep], rssend.at[0], halfsem.at[h], row, to).start()
+    pre_halves = []
+    for h, columns in enumerate(half_columns):
+        total = acc[pl.ds(pl.multiple_of(rep * BLK, BLK), BLK), columns] + selfpre[:, columns]
+        wait_for(halfrecv.at[h, pl.ds(0, REPS - 1)], halfsem.at[h])
+        for other in others:
+            total += halfrecv[h, other].astype(F32)
+        sigma = jax.nn.sigmoid(total)
+        slope = og_ref[:, columns].astype(F32) * sigma * (1.0 + total * (1.0 - sigma))
+        own[1, h] = slope.astype(BF16)
+        swap_own(1, (h,))
+        act_ref[:, columns] = (total * sigma).astype(BF16)
     slab_other()
-    act_ref[...] = (pre * sigma).astype(BF16)
+    pre_grad = jnp.concatenate([own[1, 0], own[1, 1]], axis=1)
     grad_start(0, jnp.dot(slab[rep], pre_grad, preferred_element_type=F32))
     fg_self = lax.dot_general(pre_grad, ws_ref[...], (((1,), (1,)), ((), ())), preferred_element_type=F32)
     grad_to_layer(0)
@@ -428,9 +439,10 @@
 
 def finish(act_in, fg_in, full, bias_in, act_ref, fg_ref, sg_ref, ng_ref, bg_ref):
     scale = NODES ** -0.5
+    rows = FIN // PARTS
     for a, out_ref in enumerate((sg_ref, ng_ref)):
         for h in (0, 1):
-            out_ref[:, h * HALF:(h + 1) * HALF] = full[a, h].reshape(FIN, HALF).astype(F32) * scale
+            out_ref[:, h * HALF:(h + 1) * HALF] = full[a, h].reshape(rows, HALF).astype(F32) * scale
     act_ref[...] = act_in[...]
     fg_ref[...] = fg_in[...]
     bg_ref[...] = bias_in[...] * scale
@@ -476,6 +488,9 @@
             pltpu.VMEM((8, FO), F32),
             pltpu.VMEM((REPS, 8, FO), F32),
             pltpu.VMEM((REPS, FIN, BLK), BF16),
+            pltpu.VMEM((2, REPS, BLK, HALF), BF16),
+            pltpu.VMEM((2, REPS, BLK, HALF), BF16),
+            dma((2,)),
             dma((2, 4)), dma((2, 2 * NZ)), dma((2, 2 * NZ)), dma((2, 4)),
             dma((2,)), dma((2,)), dma((2,)), dma((2,)), dma((2,)), dma((2,)),
             dma((2,)), dma((2,)), dma((2,)), dma((2,)), dma((2,)), dma((2,)),
@@ -500,8 +515,20 @@
             jax.ShapeDtypeStruct((FIN, FO), F32),
             jax.ShapeDtypeStruct((1, FO), F32),
         ),
-        in_specs=[vmem] * 4,
-        out_specs=(vmem,) * 5,
+        grid=(PARTS,),
+        in_specs=[
+            pl.BlockSpec((BLK // PARTS, FO), lambda i: (i, 0)),
+            pl.BlockSpec((BLK // PARTS, FIN), lambda i: (i, 0)),
+            pl.BlockSpec((2, 2, CHIPS // PARTS, PIECE, HALF), lambda i: (0, 0, i, 0, 0)),
+            pl.BlockSpec((1, FO), lambda i: (0, 0)),
+        ],
+        out_specs=(
+            pl.BlockSpec((BLK // PARTS, FO), lambda i: (i, 0)),
+            pl.BlockSpec((BLK // PARTS, FIN), lambda i: (i, 0)),
+            pl.BlockSpec((FIN // PARTS, FO), lambda i: (i, 0)),
+            pl.BlockSpec((FIN // PARTS, FO), lambda i: (i, 0)),
+            pl.BlockSpec((1, FO), lambda i: (0, 0)),
+        ),
         compiler_params=pltpu.CompilerParams(vmem_limit_bytes=56 * 1024 * 1024),
         name="finish",
     )(*outs)

time: 91.5 us -> 90.1 us (0.985)
  Pallas kernels: 90.7 us -> 89.3 us
    pallas_call x1, Pallas kernels: 88.1 us -> 86.9 us  [shards(): pl.pallas_call(kernel, out_shape=(jax.ShapeDtypeStruct((BLK, FO), BF16),...]
where the time goes in v5:
time: 90.1 us; the launch traced here: 90 us
  Pallas kernels  89.3 us (99%)
    pallas_call x1, Pallas kernels, shards(): pl.pallas_call(kernel, out_shape=(jax.ShapeDtypeStruct((BLK, FO), BF16),...  86.9 us
    pallas_call x1, Pallas kernels, shards(): pl.pallas_call(finish, out_shape=(jax.ShapeDtypeStruct((BLK, FO), BF16),...  2.37 us

profile of v5, /device:TPU:1, one launch (start us, length us, event | category | flops | bytes accessed | tf_op | source)
XLA Modules:
  0.0 90.0 jit_solution(6751028987457943590)
XLA Ops:
  0.6 86.9 %sage_layer.1 = (bf16[128,256]{1,0:T(8,128)(2,1)}, bf16[128,768]{1,0:T(8,128)(2,1)}, bf16[2,2,16,48,128]{4,3,2,1,0:T(8,128)(2,1)}, f32[1,256]{1,0:T(1,128)}) custom-call(bf16[128,768]{1,0:T(8,128)(2,1)} %x_hbm.1, bf16[768,256]{1,0:T(8,128)(2,1)} %ws_hbm.1, bf16[768,256]{1,0:T(8,128)(2,1)} %wn_hbm.1, f32[1,256]{1,0:T(1,128)} %bitcast.4, ...), custom_call_target="tpu_custom_call" | custom-call | flops 5000000000 | bytes 6000000 | tf_op jit(solution)/shard_map/sage_layer/pallas_call | solution.py:456
  87.6 2.4 %finish.1 = (bf16[128,256]{1,0:T(8,128)(2,1)}, bf16[128,768]{1,0:T(8,128)(2,1)}, f32[768,256]{1,0:T(8,128)}, f32[768,256]{1,0:T(8,128)}, f32[1,256]{1,0:T(1,128)}) custom-call(bf16[128,256]{1,0:T(8,128)(2,1)} %get-tuple-element.14.act_in, bf16[128,768]{1,0:T(8,128)(2,1)} %get-tuple-element.15.fg_in, bf16[2,2,16,48,128]{4,3,2,1,0:T(8,128)(2,1)} %get-tuple-element.16.full, ...), custom_call_target="tpu_custom_call" | custom-call | tf_op jit(solution)/shard_map/finish/pallas_call | solution.py:509

commit v6 on v5

--- a/solution.py
+++ b/solution.py
@@ -69,26 +69,6 @@
     def elsewhere(to_row, to_rep):
         return jnp.logical_or(to_row != row, to_rep != rep)
 
-    barrier = pltpu.get_barrier_semaphore()
-
-    def greet(to_row, to_rep):
-        pl.semaphore_signal(barrier, inc=1, device_id=(to_row, to_rep), device_id_type=MESH)
-
-    lax.fori_loop(1, REPS, lambda d, _: greet(row, lax.rem(rep + d, REPS)), None)
-    lax.fori_loop(0, REPS, lambda to, _: greet(row_at(1 - xlo, z, core), to), None)
-    lax.fori_loop(1, NZ, lambda d, _: greet(row_at(xlo, around(z + d), core), rep), None)
-    greet(sibling, rep)
-    goals = 0
-    for k in (0, 1):
-        for h in (0, 1):
-            from_row, from_rep = origin(k, h)
-
-            @pl.when(elsewhere(from_row, from_rep))
-            def _():
-                greet(from_row, from_rep)
-
-            goals += jnp.where(elsewhere(goal(k, h), goal_rep), 1, 0)
-
     inputs = [
         pltpu.make_async_copy(src, dst, insem.at[i])
         for i, (src, dst) in enumerate((
@@ -97,6 +77,27 @@
     ]
     for copy in inputs:
         copy.start()
+
+    barrier = pltpu.get_barrier_semaphore()
+
+    def greet(to_row, to_rep):
+        pl.semaphore_signal(barrier, inc=1, device_id=(to_row, to_rep), device_id_type=MESH)
+
+    goals = 0
+    for k in (0, 1):
+        for h in (0, 1):
+            from_row, from_rep = origin(k, h)
+
+            @pl.when(elsewhere(from_row, from_rep))
+            def _():
+                greet(from_row, from_rep)
+
+            goals += jnp.where(elsewhere(goal(k, h), goal_rep), 1, 0)
+    lax.fori_loop(1, REPS, lambda d, _: greet(row, lax.rem(rep + d, REPS)), None)
+    lax.fori_loop(0, REPS, lambda to, _: greet(row_at(1 - xlo, z, core), to), None)
+    lax.fori_loop(1, NZ, lambda d, _: greet(row_at(xlo, around(z + d), core), rep), None)
+    greet(sibling, rep)
+
     for copy in inputs[:2]:
         copy.wait()
 
@@ -139,8 +140,8 @@
     layer = [
         (lax.rem(xlo + dxlo, 2), lax.rem(xhi + dxhi, 2) * NY + lax.rem(y + dy, NY))
         for dxhi, dxlo, dy in (
-            (1, 0, 2), (1, 0, 1), (1, 0, 3), (1, 1, 2), (0, 1, 2), (1, 0, 0), (0, 0, 2), (1, 1, 1), (1, 1, 3),
-            (0, 1, 1), (0, 1, 3), (0, 0, 1), (0, 0, 3), (1, 1, 0), (0, 1, 0),
+            (1, 0, 2), (1, 0, 1), (1, 0, 3), (1, 0, 0), (0, 0, 2), (0, 0, 1), (0, 0, 3),
+            (1, 1, 2), (0, 1, 2), (1, 1, 1), (1, 1, 3), (0, 1, 1), (0, 1, 3), (1, 1, 0), (0, 1, 0),
         )
     ]
     mine = xlo * REPS + rep
@@ -262,20 +263,31 @@
         wait_for(slab.at[pl.ds(0, NY - 1)], slabrecv.at[1])
         wait_for(slab.at[pl.ds(0, NY - 1)], slabrecv.at[2])
 
-    def grad_start(a, part):
-        halves[a, 0] = part[:, :HALF].astype(BF16)
-        halves[a, 1] = part[:, HALF:].astype(BF16)
-        remote(halves.at[a, 1 - core], sibrecv.at[a], s1send.at[a], s1recv.at[a], sibling, rep).start()
+    def rows_for(d):
+        return pl.ds(pl.multiple_of(lax.rem(xlo + d, 2) * (FIN // 2), FIN // 2), FIN // 2)
+
+    def grad_start(a, product):
+        for d in (0, 1):
+            rows = rows_for(d)
+            part = product(rows)
+            halves[a, 0, rows, :] = part[:, :HALF].astype(BF16)
+            halves[a, 1, rows, :] = part[:, HALF:].astype(BF16)
+            remote(
+                halves.at[a, 1 - core, rows], sibrecv.at[a, rows], s1send.at[a, d], s1recv.at[a, d], sibling, rep
+            ).start()
 
     def grad_to_layer(a):
-        wait_for(sibrecv.at[a], s1recv.at[a])
-        both = halves[a, core].astype(F32) + sibrecv[a].astype(F32)
-        pieces[a] = both.astype(BF16).reshape(CHIPS, PIECE, HALF)
-        for xl, to in layer:
-            remote(
-                pieces.at[a, xl * REPS + to], piecerecv.at[a, mine], p1send.at[a], p1recv.at[a],
-                row_at(xl, z, core), to,
-            ).start()
+        for d in (0, 1):
+            rows = rows_for(d)
+            wait_for(sibrecv.at[a, rows], s1recv.at[a, d])
+            both = halves[a, core, rows, :].astype(F32) + sibrecv[a, rows, :].astype(F32)
+            owned = pl.ds(pl.multiple_of(lax.rem(xlo + d, 2) * REPS, REPS), REPS)
+            pieces[a, owned] = both.astype(BF16).reshape(REPS, PIECE, HALF)
+            for xl, to in layer[:7] if d == 0 else layer[7:]:
+                remote(
+                    pieces.at[a, xl * REPS + to], piecerecv.at[a, mine], p1send.at[a], p1recv.at[a],
+                    row_at(xl, z, core), to,
+                ).start()
 
     def grad_to_ring(a):
         total = pieces[a, mine].astype(F32)
@@ -307,7 +319,8 @@
         wait_for(full.at[a, 1 - core], s2recv.at[a])
 
     def grad_drain(a):
-        wait_for(sibrecv.at[a], s1send.at[a])
+        for d in (0, 1):
+            wait_for(sibrecv.at[a, rows_for(d)], s1send.at[a, d])
         wait_for(piecerecv.at[a, pl.ds(0, CHIPS - 1)], p1send.at[a])
         wait_for(ringrecv.at[a, pl.ds(0, NZ - 1)], r1send.at[a])
         wait_for(full.at[a, core, pl.ds(0, CHIPS - 1)], q1send.at[a])
@@ -372,7 +385,7 @@
         act_ref[:, columns] = (total * sigma).astype(BF16)
     slab_other()
     pre_grad = jnp.concatenate([own[1, 0], own[1, 1]], axis=1)
-    grad_start(0, jnp.dot(slab[rep], pre_grad, preferred_element_type=F32))
+    grad_start(0, lambda rows: jnp.dot(slab[rep, rows, :], pre_grad, preferred_element_type=F32))
     fg_self = lax.dot_general(pre_grad, ws_ref[...], (((1,), (1,)), ((), ())), preferred_element_type=F32)
     grad_to_layer(0)
 
@@ -383,15 +396,15 @@
     round_partial(1)
     slab_end()
 
-    def slab_product():
-        total = jnp.zeros((FIN, FO), F32)
+    def slab_product(rows):
+        total = jnp.zeros((FIN // 2, FO), F32)
         for pair in range(REPS // 2):
-            left = jnp.concatenate([slab[2 * pair], slab[2 * pair + 1]], axis=1)
+            left = jnp.concatenate([slab[2 * pair, rows, :], slab[2 * pair + 1, rows, :]], axis=1)
             right = psend[1, 2 * pair:2 * pair + 2].reshape(2 * BLK, FO)
             total += jnp.dot(left, right, preferred_element_type=F32)
         return total
 
-    grad_start(1, slab_product())
+    grad_start(1, slab_product)
     grad_to_layer(1)
     total = jnp.zeros((8, FO), F32)
     ones = jnp.ones((8, 2 * BLK), BF16)
@@ -493,7 +506,7 @@
             dma((2,)),
             dma((2, 4)), dma((2, 2 * NZ)), dma((2, 2 * NZ)), dma((2, 4)),
             dma((2,)), dma((2,)), dma((2,)), dma((2,)), dma((2,)), dma((2,)),
-            dma((2,)), dma((2,)), dma((2,)), dma((2,)), dma((2,)), dma((2,)),
+            dma((2, 2)), dma((2, 2)), dma((2,)), dma((2,)), dma((2,)), dma((2,)),
             dma((2,)), dma((2,)), dma((2,)), dma((2,)),
             dma, dma, dma, dma((3,)),
         ],

time: 90.1 us -> 89.1 us (0.989)
  Pallas kernels: 89.3 us -> 88.3 us
    pallas_call x1, Pallas kernels: 86.9 us -> 85.9 us  [shards(): pl.pallas_call(kernel, out_shape=(jax.ShapeDtypeStruct((BLK, FO), BF16),...]
where the time goes in v6:
time: 89.1 us; the launch traced here: 88.9 us
  Pallas kernels  88.3 us (99%)
    pallas_call x1, Pallas kernels, shards(): pl.pallas_call(kernel, out_shape=(jax.ShapeDtypeStruct((BLK, FO), BF16),...  85.9 us
    pallas_call x1, Pallas kernels, shards(): pl.pallas_call(finish, out_shape=(jax.ShapeDtypeStruct((BLK, FO), BF16),...  2.37 us

profile of v6, /device:TPU:1, one launch (start us, length us, event | category | flops | bytes accessed | tf_op | source)
XLA Modules:
  0.0 88.9 jit_solution(15190564767456854287)
XLA Ops:
  0.6 85.9 %sage_layer.1 = (bf16[128,256]{1,0:T(8,128)(2,1)}, bf16[128,768]{1,0:T(8,128)(2,1)}, bf16[2,2,16,48,128]{4,3,2,1,0:T(8,128)(2,1)}, f32[1,256]{1,0:T(1,128)}) custom-call(bf16[128,768]{1,0:T(8,128)(2,1)} %x_hbm.1, bf16[768,256]{1,0:T(8,128)(2,1)} %ws_hbm.1, bf16[768,256]{1,0:T(8,128)(2,1)} %wn_hbm.1, f32[1,256]{1,0:T(1,128)} %bitcast.4, ...), custom_call_target="tpu_custom_call" | custom-call | flops 5000000000 | bytes 6000000 | tf_op jit(solution)/shard_map/sage_layer/pallas_call | solution.py:469
  86.6 2.4 %finish.1 = (bf16[128,256]{1,0:T(8,128)(2,1)}, bf16[128,768]{1,0:T(8,128)(2,1)}, f32[768,256]{1,0:T(8,128)}, f32[768,256]{1,0:T(8,128)}, f32[1,256]{1,0:T(1,128)}) custom-call(bf16[128,256]{1,0:T(8,128)(2,1)} %get-tuple-element.14.act_in, bf16[128,768]{1,0:T(8,128)(2,1)} %get-tuple-element.15.fg_in, bf16[2,2,16,48,128]{4,3,2,1,0:T(8,128)(2,1)} %get-tuple-element.16.full, ...), custom_call_target="tpu_custom_call" | custom-call | tf_op jit(solution)/shard_map/finish/pallas_call | solution.py:522

commit v7 on v6

--- a/solution.py
+++ b/solution.py
@@ -307,13 +307,16 @@
             total += ringrecv[a, zz].astype(F32)
         full[a, core, mine] = total.astype(BF16)
         piece = full.at[a, core, mine]
-        for xl, to in layer:
-            remote(piece, piece, q1send.at[a], q1recv.at[a], row_at(xl, z, core), to).start()
+        for d in (0, 1):
+            for xl, to in layer[:7] if d == 0 else layer[7:]:
+                remote(piece, piece, q1send.at[a], q1recv.at[a, d], row_at(xl, z, core), to).start()
 
     def grad_share(a):
-        wait_for(full.at[a, core, pl.ds(0, CHIPS - 1)], q1recv.at[a])
-        half = full.at[a, core]
-        remote(half, half, s2send.at[a], s2recv.at[a], sibling, rep).start()
+        for d in (0, 1):
+            wait_for(full.at[a, core, pl.ds(0, REPS - 1 + d)], q1recv.at[a, d])
+            owned = pl.ds(pl.multiple_of(lax.rem(xlo + d, 2) * REPS, REPS), REPS)
+            part = full.at[a, core, owned]
+            remote(part, part, s2send.at[a], s2recv.at[a], sibling, rep).start()
 
     def grad_end(a):
         wait_for(full.at[a, 1 - core], s2recv.at[a])
@@ -507,7 +510,7 @@
             dma((2, 4)), dma((2, 2 * NZ)), dma((2, 2 * NZ)), dma((2, 4)),
             dma((2,)), dma((2,)), dma((2,)), dma((2,)), dma((2,)), dma((2,)),
             dma((2, 2)), dma((2, 2)), dma((2,)), dma((2,)), dma((2,)), dma((2,)),
-            dma((2,)), dma((2,)), dma((2,)), dma((2,)),
+            dma((2,)), dma((2, 2)), dma((2,)), dma((2,)),
             dma, dma, dma, dma((3,)),
         ],
         compiler_params=pltpu.CompilerParams(

time: 89.1 us -> 89 us (level)
  no operation moved by 1% of the time
where the time goes in v7:
time: 89 us; the launch traced here: 88.8 us
  Pallas kernels  88.2 us (99%)
    pallas_call x1, Pallas kernels, shards(): pl.pallas_call(kernel, out_shape=(jax.ShapeDtypeStruct((BLK, FO), BF16),...  85.8 us
    pallas_call x1, Pallas kernels, shards(): pl.pallas_call(finish, out_shape=(jax.ShapeDtypeStruct((BLK, FO), BF16),...  2.37 us

profile of v7, /device:TPU:1, one launch (start us, length us, event | category | flops | bytes accessed | tf_op | source)
XLA Modules:
  0.0 88.8 jit_solution(15326667899434870193)
XLA Ops:
  0.6 85.8 %sage_layer.1 = (bf16[128,256]{1,0:T(8,128)(2,1)}, bf16[128,768]{1,0:T(8,128)(2,1)}, bf16[2,2,16,48,128]{4,3,2,1,0:T(8,128)(2,1)}, f32[1,256]{1,0:T(1,128)}) custom-call(bf16[128,768]{1,0:T(8,128)(2,1)} %x_hbm.1, bf16[768,256]{1,0:T(8,128)(2,1)} %ws_hbm.1, bf16[768,256]{1,0:T(8,128)(2,1)} %wn_hbm.1, f32[1,256]{1,0:T(1,128)} %bitcast.4, ...), custom_call_target="tpu_custom_call" | custom-call | flops 5000000000 | bytes 6000000 | tf_op jit(solution)/shard_map/sage_layer/pallas_call | solution.py:472
  86.4 2.4 %finish.1 = (bf16[128,256]{1,0:T(8,128)(2,1)}, bf16[128,768]{1,0:T(8,128)(2,1)}, f32[768,256]{1,0:T(8,128)}, f32[768,256]{1,0:T(8,128)}, f32[1,256]{1,0:T(1,128)}) custom-call(bf16[128,256]{1,0:T(8,128)(2,1)} %get-tuple-element.14.act_in, bf16[128,768]{1,0:T(8,128)(2,1)} %get-tuple-element.15.fg_in, bf16[2,2,16,48,128]{4,3,2,1,0:T(8,128)(2,1)} %get-tuple-element.16.full, ...), custom_call_target="tpu_custom_call" | custom-call | tf_op jit(solution)/shard_map/finish/pallas_call | solution.py:525

commit v8 on v6

--- a/solution.py
+++ b/solution.py
@@ -383,11 +383,11 @@
         own[1, h] = slope.astype(BF16)
         swap_own(1, (h,))
         act_ref[:, columns] = (total * sigma).astype(BF16)
-    slab_other()
     pre_grad = jnp.concatenate([own[1, 0], own[1, 1]], axis=1)
     grad_start(0, lambda rows: jnp.dot(slab[rep, rows, :], pre_grad, preferred_element_type=F32))
     fg_self = lax.dot_general(pre_grad, ws_ref[...], (((1,), (1,)), ((), ())), preferred_element_type=F32)
     grad_to_layer(0)
+    slab_other()
 
     gather(1, {
         "stepped": lambda: grad_to_ring(0),

time: 89.1 us -> 89.4 us (level)
  no operation moved by 1% of the time
where the time goes in v8:
time: 89.4 us; the launch traced here: 89.3 us
  Pallas kernels  88.6 us (99%)
    pallas_call x1, Pallas kernels, shards(): pl.pallas_call(kernel, out_shape=(jax.ShapeDtypeStruct((BLK, FO), BF16),...  86.2 us
    pallas_call x1, Pallas kernels, shards(): pl.pallas_call(finish, out_shape=(jax.ShapeDtypeStruct((BLK, FO), BF16),...  2.37 us

profile of v8, /device:TPU:1, one launch (start us, length us, event | category | flops | bytes accessed | tf_op | source)
XLA Modules:
  0.0 89.3 jit_solution(6639908971685416737)
XLA Ops:
  0.6 86.2 %sage_layer.1 = (bf16[128,256]{1,0:T(8,128)(2,1)}, bf16[128,768]{1,0:T(8,128)(2,1)}, bf16[2,2,16,48,128]{4,3,2,1,0:T(8,128)(2,1)}, f32[1,256]{1,0:T(1,128)}) custom-call(bf16[128,768]{1,0:T(8,128)(2,1)} %x_hbm.1, bf16[768,256]{1,0:T(8,128)(2,1)} %ws_hbm.1, bf16[768,256]{1,0:T(8,128)(2,1)} %wn_hbm.1, f32[1,256]{1,0:T(1,128)} %bitcast.4, ...), custom_call_target="tpu_custom_call" | custom-call | flops 5000000000 | bytes 6000000 | tf_op jit(solution)/shard_map/sage_layer/pallas_call | solution.py:469
  86.9 2.4 %finish.1 = (bf16[128,256]{1,0:T(8,128)(2,1)}, bf16[128,768]{1,0:T(8,128)(2,1)}, f32[768,256]{1,0:T(8,128)}, f32[768,256]{1,0:T(8,128)}, f32[1,256]{1,0:T(1,128)}) custom-call(bf16[128,256]{1,0:T(8,128)(2,1)} %get-tuple-element.14.act_in, bf16[128,768]{1,0:T(8,128)(2,1)} %get-tuple-element.15.fg_in, bf16[2,2,16,48,128]{4,3,2,1,0:T(8,128)(2,1)} %get-tuple-element.16.full, ...), custom_call_target="tpu_custom_call" | custom-call | tf_op jit(solution)/shard_map/finish/pallas_call | solution.py:522
